TPU v7x, 128 devices: a whole 4x4x4 slice. The times are simulated.
128 devices in a mesh: seq: 32 (over x, y, z_hi), sp: 4 (over z_lo, core).
Axes of the slice: x: 4, y: 4, z: 4 (z_hi: 2, z_lo: 2; z = z_hi * 2 + z_lo), core: 2. Of those that a mesh axis runs over, the one named last changes fastest.
Arguments:
- group_hidden: bfloat16 [384, 5120], P('seq', 'sp'), may hold values from -30 to 30
- queries: bfloat16 [384, 5120], P('seq', 'sp'), may hold values from -18 to 18
- history_keys: bfloat16 [65536, 5120], P('seq', 'sp'), may hold values from -6 to 6
- history_values: bfloat16 [65536, 5120], P('seq', 'sp'), may hold values from -16 to 16
- valid_len: int32 [32], P('seq'), may hold values from 512 to 2048, as said below
- out_weight: bfloat16 [5120, 5120], P('sp', 'seq'), may hold values from -0.078125 to 0.078125
- attn_gate: float32 [5120], P('sp'), may hold values from 0.5 to 1.5
- head_gain: float32 [5120], replicated, may hold values from 0.25 to 1.75
- head_shift: float32 [5120], replicated, may hold values from -6 to 6
- head_weight: float32 [5120, 64], replicated, may hold values from -0.078125 to 0.078125
- head_bias: float32 [64], replicated, may hold values from -6 to 6
- noisy_latent: float32 [64, 24, 16], P('seq', 'sp'), may hold values from -6 to 6
- prev_latent: bfloat16 [2, 64, 24, 16], P(None, 'seq', 'sp'), may hold values from -6 to 6
- prev_feat: bfloat16 [2, 64, 24, 384], P(None, 'seq', 'sp'), may hold values from -6 to 6
- conv_in_weight: bfloat16 [3, 3, 3, 16, 384], replicated, may hold values from -0.3125 to 0.3125
- conv_in_bias: float32 [384], replicated, may hold values from -6 to 6
- vae_gain: float32 [384], replicated, may hold values from 0.25 to 1.75
- conv_mid_weight: bfloat16 [3, 3, 3, 384, 384], replicated, may hold values from -0.0625 to 0.0625
- conv_mid_bias: float32 [384], replicated, may hold values from -6 to 6
Outputs:
- hidden_out: bfloat16 [384, 5120], P('seq', 'sp')
- decoded: float32 [64, 24, 384], P('seq', 'sp')
Inputs may be any that keep to these rules, and one draw needn't show every extreme that they name: `valid_len`: every block has at least 512 visible positions; some block is fully visible.
All inputs are finite; a program needn't handle non-finite values.
Results may differ from a plain program's by a relative error of at most 0.0085.
Values may be sent and summed in bfloat16 or wider, within the bound.
A program may use at most 320 MiB of HBM per device.

v0:
```python
import math

import jax
import jax.numpy as jnp
from jax import lax
from jax.sharding import PartitionSpec as P

D = 5120
HD = 128


noise_level = 0.75


def with_halo(value, sides, width):
    for axis, dim in sides:
        size, length = (lax.axis_size(axis), value.shape[dim])
        up = [(i, (i + 1) % size) for i in range(size - 1)]
        down = [(j, i) for i, j in up]
        last = lax.slice_in_dim(value, length - width, length, axis=dim)
        first = lax.slice_in_dim(value, 0, width, axis=dim)
        before = lax.ppermute(last, axis, up)
        after = lax.ppermute(first, axis, down)
        value = jnp.concatenate([before, value, after], axis=dim)
    return value


def joined(value, axis, join):
    pieces = jax.tree.map(lambda part: lax.all_gather(part, axis), value)
    head = jax.tree.map(lambda part: part[0], pieces)
    tail = jax.tree.map(lambda part: part[1:], pieces)
    so_far, _ = lax.scan(lambda so_far, share: (join(so_far, share), None), head, tail)
    return so_far


def widen(factor, head_size):
    return jnp.repeat(factor, head_size, axis=1)


def join_partials(first_part, second_part):
    best_a, total_a, accum_a = first_part
    best_b, total_b, accum_b = second_part
    best = jnp.maximum(best_a, best_b)
    scale_a = jnp.exp(best_a - best)
    scale_b = jnp.exp(best_b - best)
    total = total_a * scale_a + total_b * scale_b
    accum = accum_a * widen(scale_a, HD) + accum_b * widen(scale_b, HD)
    return (best, total, accum)


def causal_conv(earlier, current, weight, bias):
    frames = jnp.concatenate([earlier, current[None]], axis=0)
    padded = with_halo(frames, (("seq", 1), ("sp", 2)), 1)
    row_count, col_count = (current.shape[0], current.shape[1])
    tap_list = [
        padded[step_t, shift_h : shift_h + row_count, shift_w : shift_w + col_count, :]
        for step_t in range(3)
        for shift_h in range(3)
        for shift_w in range(3)
    ]
    columns = jnp.concatenate(tap_list, axis=-1).reshape(row_count * col_count, -1)
    result = (
        jnp.dot(columns, weight.reshape(-1, weight.shape[-1]), preferred_element_type=jnp.float32)
        + bias
    )
    return result.reshape(row_count, col_count, -1)


def local(
    group_hidden,
    queries,
    history_keys,
    history_values,
    valid_len,
    out_weight,
    attn_gate,
    head_gain,
    head_shift,
    head_weight,
    head_bias,
    noisy_latent,
    prev_latent,
    prev_feat,
    conv_in_weight,
    conv_in_bias,
    vae_gain,
    conv_mid_weight,
    conv_mid_bias,
):
    own_tokens, local_width = group_hidden.shape
    head_count = local_width // HD
    scale = 1.0 / math.sqrt(HD)
    all_queries = lax.all_gather(queries, "seq", axis=0, tiled=True)
    query_total = all_queries.shape[0]
    visible = (jnp.arange(history_keys.shape[0], dtype=jnp.int32) < valid_len[0])[None, :]

    def one_head(head_index, state_now):
        best_all, total_all, accum_all = state_now
        col_start = head_index * HD
        query_head = lax.dynamic_slice_in_dim(all_queries, col_start, HD, 1)
        key_head = lax.dynamic_slice_in_dim(history_keys, col_start, HD, 1)
        value_head = lax.dynamic_slice_in_dim(history_values, col_start, HD, 1)
        scores = (
            lax.dot_general(
                query_head, key_head, (((1,), (1,)), ((), ())), preferred_element_type=jnp.float32
            )
            * scale
        )
        scores = jnp.where(visible, scores, -1e30)
        block_max = jnp.max(scores, axis=-1, keepdims=True)
        weights = jnp.where(visible, jnp.exp(scores - block_max), 0.0).astype(jnp.bfloat16)
        block_sum = jnp.sum(weights.astype(jnp.float32), axis=-1, keepdims=True)
        block_acc = jnp.dot(weights, value_head, preferred_element_type=jnp.float32)
        best_all = lax.dynamic_update_slice_in_dim(best_all, block_max, head_index, 1)
        total_all = lax.dynamic_update_slice_in_dim(total_all, block_sum, head_index, 1)
        accum_all = lax.dynamic_update_slice_in_dim(accum_all, block_acc, col_start, 1)
        return (best_all, total_all, accum_all)

    start_state = (
        jnp.zeros((query_total, head_count), jnp.float32),
        jnp.zeros((query_total, head_count), jnp.float32),
        jnp.zeros((query_total, local_width), jnp.float32),
    )
    best_all, total_all, accum_all = lax.fori_loop(0, head_count, one_head, start_state)
    best, total, accum = joined((best_all, total_all, accum_all), "seq", join_partials)
    attn_all = (accum / widen(total, HD)).astype(jnp.bfloat16)
    token_part = jnp.dot(attn_all, out_weight, preferred_element_type=jnp.float32)
    partial_terms = lax.all_to_all(token_part, "seq", split_axis=0, concat_axis=1, tiled=True)
    projected = lax.psum_scatter(partial_terms, "sp", scatter_dimension=1, tiled=True)
    updated = group_hidden.astype(jnp.float32) + attn_gate * projected
    hidden_out = updated.astype(jnp.bfloat16)
    feat_start = lax.axis_index("sp") * local_width
    gain_local = lax.dynamic_slice_in_dim(head_gain, feat_start, local_width, 0)
    shift_local = lax.dynamic_slice_in_dim(head_shift, feat_start, local_width, 0)
    weight_rows = lax.dynamic_slice_in_dim(head_weight, feat_start, local_width, 0)
    first_sum = jnp.sum(updated, axis=-1)
    square_sum = jnp.sum(updated * updated, axis=-1)
    first_sum, square_sum = lax.psum((first_sum, square_sum), "sp")
    mean_val = (first_sum / D)[:, None]
    var_val = (square_sum / D)[:, None] - mean_val * mean_val
    normed = (updated - mean_val) * lax.rsqrt(var_val + 1e-06) * gain_local + shift_local
    head_part = jnp.dot(
        normed, weight_rows, precision=lax.Precision.HIGHEST, preferred_element_type=jnp.float32
    )
    velocity = lax.psum_scatter(head_part, "sp", scatter_dimension=0, tiled=True) + head_bias
    patch_count = velocity.shape[0]
    velocity = (
        velocity.reshape(patch_count, 2, 2, -1)
        .transpose(1, 0, 2, 3)
        .reshape(2, 2 * patch_count, -1)
    )
    clean = (noisy_latent - noise_level * velocity).astype(jnp.bfloat16)
    first = causal_conv(prev_latent, clean, conv_in_weight, conv_in_bias)
    norm_scale = lax.rsqrt(jnp.mean(first * first, axis=-1, keepdims=True) + 1e-06)
    activated = jax.nn.silu(first * norm_scale * vae_gain).astype(jnp.bfloat16)
    decoded = first + causal_conv(prev_feat, activated, conv_mid_weight, conv_mid_bias)
    return (hidden_out, decoded)


def solution(mesh):
    placed = (
        P("seq", "sp"),
        P("seq", "sp"),
        P("seq", "sp"),
        P("seq", "sp"),
        P("seq"),
        P("sp", "seq"),
        P("sp"),
        P(),
        P(),
        P(),
        P(),
        P("seq", "sp", None),
        P(None, "seq", "sp", None),
        P(None, "seq", "sp", None),
        P(),
        P(),
        P(),
        P(),
        P(),
    )
    return jax.shard_map(
        local,
        mesh=mesh,
        in_specs=placed,
        out_specs=(P("seq", "sp"), P("seq", "sp", None)),
        check_vma=False,
    )
```

profile of v0, /device:TPU:3, one launch (start us, length us, event | category | flops | bytes accessed | tf_op | source)
XLA Modules:
  0.0 1055.2 jit_solution(2523793354641094514)
XLA Ops:
  7.2 78.4 %all-gather.3 = bf16[32,12,1280]{2,1,0:T(8,128)(2,1)S(1)} all-gather(bf16[1,12,1280]{2,1,0:T(8,128)(2,1)} %bitcast.69), channel_id=1, replica_groups=mesh['seq'=32,'sp'=4] {'seq'}, dimensions={0}, use_global_device_ids=true | all-gather | bytes 1013760 | tf_op jit(solution)/shard_map/all_gather | solution.py:93
  86.9 49.9 %while.33 = (s32[]{:T(128)}, f32[384,10]{0,1:T(8,128)S(1)}, f32[384,10]{0,1:T(8,128)S(1)}, f32[384,1280]{1,0:T(8,128)S(1)}, bf16[384,1280]{1,0:T(8,128)(2,1)}, /...) while((s32[]{:T(128)}, f32[384,10]{0,1:T(8,128)S(1)}, ...), condition=%wide.region_3.4_spmd.clone, body=%wide.region_0.3_spmd.clone.sunk | while | flops 411305216 | bytes 10810031 | solution.py:124
  138.1 78.1 %all-gather = f32[12288,10]{0,1:T(8,128)S(1)} all-gather(f32[384,10]{0,1:T(8,128)S(1)} %get-tuple-element.181), channel_id=2, replica_groups=mesh['seq'=32,'sp'=4] {'seq'}, dimensions={0}, use_global_device_ids=true | all-gather | bytes 506880 | tf_op jit(solution)/shard_map/all_gather | solution.py:29
  217.2 86.6 %all-gather.1 = f32[12288,10]{0,1:T(8,128)S(1)} all-gather(f32[384,10]{0,1:T(8,128)S(1)} %get-tuple-element.182), channel_id=3, replica_groups=mesh['seq'=32,'sp'=4] {'seq'}, dimensions={0}, use_global_device_ids=true | all-gather | bytes 506880 | tf_op jit(solution)/shard_map/all_gather | solution.py:29
  306.6 318.1 %all-gather.6.cloned.1.call-done = f32[12288,1280]{1,0:T(8,128)} async-done(((f32[384,1280]{1,0:T(8,128)}), f32[12288,1280]{1,0:T(8,128)}) %all-gather.6.cloned.1.call-update) | async-done | bytes 62914576 | tf_op jit(solution)/shard_map/all_gather | solution.py:29
  628.0 40.4 %slice.323 = f32[11904,1280]{1,0:T(8,128)} slice(f32[12288,1280]{1,0:T(8,128)} %all-gather.6.cloned.1.call-done), slice={[384:12288], [0:1280]} | slice | bytes 121896960 | tf_op jit(solution)/shard_map/slice | solution.py:31
  668.4 278.1 %while.32 = (s32[]{:T(128)}, f32[384,10]{0,1:T(8,128)S(1)}, f32[384,10]{0,1:T(8,128)S(1)}, f32[384,1280]{0,1:T(8,128)}, f32[31,384,10]{1,0,2:T(8,128)}, /*index=...) while((s32[]{:T(128)}, f32[384,10]{0,1:T(8,128)S(1)}, f32[384,10]{0,1:T(8,128)S(1)}, ...), condition=%wide.region_5.6_spmd, body=%wide.region_4.5_spmd.sunk | while | flops 1497602 | bytes 13977693 | solution.py:32
  669.5 3.0 constant_dynamic-slice_fusion.6
  674.3 3.1 fusion.51
  678.4 3.0 constant_dynamic-slice_fusion.6
  683.3 3.1 fusion.51
  687.4 3.0 constant_dynamic-slice_fusion.6
  692.3 3.1 fusion.51
  696.4 3.0 constant_dynamic-slice_fusion.6
  701.2 3.1 fusion.51
  705.3 3.0 constant_dynamic-slice_fusion.6
  710.2 3.1 fusion.51
  714.3 3.0 constant_dynamic-slice_fusion.6
  719.2 3.1 fusion.51
  723.3 3.0 constant_dynamic-slice_fusion.6
  728.2 3.1 fusion.51
  732.2 3.0 constant_dynamic-slice_fusion.6
  737.1 3.1 fusion.51
  741.2 3.0 constant_dynamic-slice_fusion.6
  746.1 3.1 fusion.51
  755.1 3.1 fusion.51
  764.0 3.1 fusion.51
  768.1 3.0 constant_dynamic-slice_fusion.6
  773.0 3.1 fusion.51
  782.0 3.1 fusion.51
  790.9 3.1 fusion.51
  795.0 3.0 constant_dynamic-slice_fusion.6
  799.9 3.1 fusion.51
  808.9 3.1 fusion.51
  817.8 3.1 fusion.51
  821.9 3.0 constant_dynamic-slice_fusion.6
  826.8 3.1 fusion.51
  835.8 3.1 fusion.51
  844.8 3.1 fusion.51
  848.9 3.0 constant_dynamic-slice_fusion.6
  853.7 3.1 fusion.51
  862.7 3.1 fusion.51
  871.7 3.1 fusion.51
  875.8 3.0 constant_dynamic-slice_fusion.6
  880.6 3.1 fusion.51
  889.6 3.1 fusion.51
  898.6 3.1 fusion.51
  902.7 3.0 constant_dynamic-slice_fusion.6
  907.5 3.1 fusion.51
  916.5 3.1 fusion.51
  925.5 3.1 fusion.51
  934.5 3.1 fusion.51
  938.5 3.0 constant_dynamic-slice_fusion.6
  943.4 3.1 fusion.51
  950.3 15.0 %all_to_all.19 = f32[32,1,1920]{2,1,0:T(1,128)S(1)} all-to-all(f32[32,1,1920]{2,1,0:T(1,128)S(1)} %reshape.232), channel_id=1, replica_groups=mesh['seq'=32,'sp'=4] {'seq'}, dimensions={0} | all-to-all | bytes 491520 | tf_op jit(solution)/shard_map/all_to_all | solution.py:128
  971.4 14.8 %reduce-scatter.2.cloned.1.call-done = f32[12,1280]{1,0:T(8,128)} async-done(((f32[12,5120]{1,0:T(8,128)}), f32[12,1280]{1,0:T(8,128)}) %reduce-scatter.2.cloned.1.call-update) | async-done | bytes 61456 | tf_op jit(solution)/shard_map/reduce_scatter | solution.py:129
  987.9 5.2 all-reduce.1
  994.4 6.2 all-reduce
  1000.7 4.8 collective-permute-start
  1005.6 5.0 collective-permute-start.1
  1011.7 4.9 collective-permute-start.2
  1022.8 4.8 collective-permute-start.4
  1027.7 6.1 collective-permute-start.5
  1043.3 4.4 fusion.14
  (424 shorter events, 222.4 us)
Async XLA Ops:
  7.2 985.9 %copy-start = (f32[5120,64]{0,1:T(8,128)S(1)}, f32[5120,64]{0,1:T(8,128)}, u32[]{:S(2)}) copy-start(f32[5120,64]{0,1:T(8,128)} %param.32) | copy-start | bytes 3932164
  7.2 617.5 %all-gather.6.cloned.1.call-start = ((), (), s32[]{:S(2)}) async-start(), calls=%async_computation.3 | async-start | bytes 64880640 | tf_op jit(solution)/shard_map/all_gather | solution.py:29
  136.8 1.3 copy-start.1
  138.1 848.2 %reduce-scatter.2.cloned.1.call-start = ((), (), s32[]{:S(2)}) async-start(), calls=%async_computation.2 | async-start | bytes 409600 | tf_op jit(solution)/shard_map/reduce_scatter | solution.py:129
  216.3 0.9 copy-start.2
  303.8 0.9 copy-start.3
  624.6 1.5 slice-start
  628.0 40.4 %slice-start.1 = ((f32[12288,10]{0,1:T(8,128)}), f32[384,10]{0,1:T(8,128)S(1)}, s32[]{:S(2)}) async-start(f32[12288,10]{0,1:T(8,128)} %copy-done.2), calls=%async_computation.5 | async-start | bytes 49152 | tf_op jit(solution)/shard_map/slice | solution.py:30
  628.0 40.4 %slice-start.2 = ((f32[12288,10]{0,1:T(8,128)}), f32[384,10]{0,1:T(8,128)S(1)}, s32[]{:S(2)}) async-start(f32[12288,10]{0,1:T(8,128)} %copy-done.3), calls=%async_computation.6 | async-start | bytes 49152 | tf_op jit(solution)/shard_map/slice | solution.py:30
  949.7 20.5 %copy-start.14 = (u32[128]{0:T(128)S(1)}, u32[128]{0:T(128)}, u32[]{:S(2)}) copy-start(u32[128]{0:T(128)} %constant.105) | copy-start | bytes 1540
  949.7 36.6 %copy-start.5 = (bf16[12,1280]{1,0:T(8,128)(2,1)S(1)}, bf16[12,1280]{1,0:T(8,128)(2,1)}, u32[]{:S(2)}) copy-start(bf16[12,1280]{1,0:T(8,128)(2,1)} %param.23) | copy-start | bytes 92164
  949.7 36.6 %copy-start.8 = (f32[1280]{0:T(1024)S(1)}, f32[1280]{0:T(1024)}, u32[]{:S(2)}) copy-start(f32[1280]{0:T(1024)} %param.29) | copy-start | bytes 15364
  949.7 50.9 %copy-start.13 = (f32[64]{0:T(128)S(1)}, f32[64]{0:T(128)}, u32[]{:S(2)}) copy-start(f32[64]{0:T(128)} %param.33) | copy-start | bytes 772
  949.7 51.0 %copy-start.10 = (f32[2,6,16]{2,0,1:T(2,128)S(1)}, f32[2,6,16]{2,0,1:T(2,128)}, u32[]{:S(2)}) copy-start(f32[2,6,16]{2,0,1:T(2,128)} %param.34) | copy-start | bytes 2308
  949.7 51.0 %copy-start.6 = (bf16[2,2,6,16]{3,1,2,0:T(2,128)(2,1)S(1)}, bf16[2,2,6,16]{3,1,2,0:T(2,128)(2,1)}, u32[]{:S(2)}) copy-start(bf16[2,2,6,16]{3,1,2,0:T(2,128)(2,1)} %param.35) | copy-start | bytes 2308
  949.7 60.8 %copy-start.7 = (bf16[2,2,6,384]{3,1,2,0:T(2,128)(2,1)S(1)}, bf16[2,2,6,384]{3,1,2,0:T(2,128)(2,1)}, u32[]{:S(2)}) copy-start(bf16[2,2,6,384]{3,1,2,0:T(2,128)(2,1)} %param.36) | copy-start | bytes 55300
  949.8 60.8 %slice-start.3 = ((bf16[2,2,6,16]{3,1,2,0:T(2,128)(2,1)}), bf16[1,2,6,16]{3,1,2,0:T(2,128)(2,1)S(1)}, s32[]{:S(2)}) async-start(bf16[2,2,6,16]{3,1,2,0:T(2,128)(2,1)} %param.35), calls=%async_computation.7 | async-start | bytes 6144 | tf_op jit(solution)/shard_map/slice | solution.py:56
  949.8 72.4 %copy-start.4 = (bf16[3,3,3,16,384]{4,3,2,1,0:T(8,128)(2,1)S(1)}, bf16[3,3,3,16,384]{4,3,2,1,0:T(8,128)(2,1)}, u32[]{:S(2)}) copy-start(bf16[3,3,3,16,384]{4,3,2,1,0:T(8,128)(2,1)} %param.37) | copy-start | bytes 995332
  949.8 72.4 %copy-start.11 = (f32[384]{0:T(512)S(1)}, f32[384]{0:T(512)}, u32[]{:S(2)}) copy-start(f32[384]{0:T(512)} %param.38) | copy-start | bytes 4612
  950.3 72.3 %copy-start.9 = (f32[384]{0:T(512)S(1)}, f32[384]{0:T(512)}, u32[]{:S(2)}) copy-start(f32[384]{0:T(512)} %param.39) | copy-start | bytes 4612
  967.6 75.6 %copy-start.12 = (f32[384]{0:T(512)S(1)}, f32[384]{0:T(512)}, u32[]{:S(2)}) copy-start(f32[384]{0:T(512)} %param.41) | copy-start | bytes 4612
  1000.7 9.9 collective-permute-start
  1005.6 5.9 collective-permute-start.1
  1011.7 6.9 collective-permute-start.2
  1016.6 4.9 collective-permute-start.3
  1022.8 11.1 %collective-permute-start.4 = (bf16[3,1,6,384]{3,1,2,0:T(2,128)(2,1)S(1)}, bf16[3,1,6,384]{3,1,2,0:T(2,128)(2,1)S(1)}, u32[]{:S(2)}, u32[]{:S(2)}) collective-permute-start(bf16[3,1,6,384]{3,1,2,0:T(2,128)(2,1)S(1)} %get-tuple-element.315), channel_id=1, source_target_pairs={{0,4},{4,8},{8,12},{12,16},{16,20},{20,24},{24,28},{28,32},{32,36}... | collective-permute-start | bytes 41480 | tf_op jit(solution)/shard_map/ppermute | solution.py:22
  1027.7 7.1 collective-permute-start.5
  1034.8 4.7 collective-permute-start.6
  1037.0 5.0 collective-permute-start.7
Sparse Core Ops, SparseCore 0:
  138.2 486.3 all-gather.5
  968.7 17.4 reduce-scatter.1
where the time goes:
time: 1060 us
  waiting for transfers between devices  340 us (32%)
  blocking collectives  270 us (25%)
  local copies, waits for them, and re-layouts  240 us (23%)
  other arithmetic  115 us (11%)
  matrix products  42.2 us (4%)
  starting transfers between devices  32 us (3%)
  between operations  15.9 us (2%)
    all_gather x1, waiting for transfers between devices, joined(): pieces = jax.tree.map(lambda part: lax.all_gather(part, axis), value)  318 us
    dynamic_slice x93, local copies, waits for them, and re-layouts, joined(): lax.scan(lambda so_far, share: (join(so_far, share), None), head, tail)  181 us
    all_gather x2, blocking collectives, joined(): pieces = jax.tree.map(lambda part: lax.all_gather(part, axis), value)  165 us
    add x31, other arithmetic, join_partials(): accum = accum_a * widen(scale_a, HD) + accum_b * widen(scale_b, HD)  95.3 us
    all_gather x1, blocking collectives, local(): all_queries = lax.all_gather(queries, 'seq', axis=0, tiled=True)  78.4 us
    slice x5, local copies, waits for them, and re-layouts, joined(): tail = jax.tree.map(lambda part: part[1:], pieces)  42.4 us
  transfers between devices with their start and end apart: 10, of which 6 were waited for; matrix products, arithmetic and copies ran while one was open for 0% of the time, Pallas kernels for 0%

commit v1 on v0

v1 whole, which is shorter than its diff:
```python
import functools
import math

import jax
import jax.numpy as jnp
from jax import lax
from jax.experimental import pallas as pl
from jax.experimental.pallas import tpu as pltpu
from jax.sharding import PartitionSpec as P

MESH = pl.DeviceIdType.MESH
BF16 = jnp.bfloat16
F32 = jnp.float32

D = 5120
HD = 128
NSEQ = 32
NSP = 4
TOK = 12
PAD = 16
TOKENS = NSEQ * TOK
HIST = 2048
FEAT = 1280
COLS = 160
CH = 5
CW = FEAT // CH
VAE = 384
EXP2_SCALE = math.log2(math.e) / math.sqrt(HD)
NOISE = 0.75


def iota(shape, dim):
    return lax.broadcasted_iota(jnp.int32, shape, dim)


def wait_bytes(region, sem):
    pltpu.make_async_copy(region, region, sem).wait()


def pad_rows(rows):
    width = rows.shape[-1]
    pairs = rows.reshape(-1, 2 * TOK, width)
    even = pairs[:, :PAD]
    odd = pltpu.roll(pairs, TOK, 1)[:, :PAD]
    return jnp.concatenate([even[:, None], odd[:, None]], axis=1).reshape(-1, PAD, width)


def pack_rows(blocks):
    width = blocks.shape[-1]
    pairs = blocks.reshape(-1, 2, PAD, width)
    zeros = jnp.zeros((pairs.shape[0], 8, width), F32)
    even = jnp.concatenate([pairs[:, 0], zeros], axis=1)
    odd = pltpu.roll(jnp.concatenate([pairs[:, 1], zeros], axis=1), TOK, 1)
    row = iota(even.shape, 1)
    return jnp.where(row < TOK, even, odd).reshape(-1, width)


def kernel(
    hidden_ref,
    q_ref,
    k_hbm,
    v_hbm,
    valid_ref,
    w_hbm,
    rows_ref,
    vecs_ref,
    bias_ref,
    headw_hbm,
    noisy_ref,
    platent_ref,
    pfeat_ref,
    win_hbm,
    wmid_hbm,
    hidden_out,
    decoded_out,
    k_s,
    v_s,
    w_s,
    headw_s,
    win_s,
    wmid_s,
    qs,
    qg,
    pc,
    rc,
    ao,
    ag,
    es,
    er,
    gs,
    gr,
    ls,
    lr,
    fs,
    fr,
    fpad,
    cells,
    vtok,
    vcell,
    feats,
    firsts,
    acts,
    proj,
    upd,
    ksem,
    vsem,
    wsem,
    lsem,
    q_send,
    q_recv,
    c_send,
    c_recv,
    d_send,
    d_recv,
    e_send,
    e_recv,
    g_send,
    g_recv,
    l_send,
    l_recv,
    f_send,
    f_recv,
):
    s = lax.axis_index("seq")
    p = lax.axis_index("sp")
    owner_sp = s // 8
    piece = lax.rem(s, 8)

    barrier = pltpu.get_barrier_semaphore()

    def greet(to_s, to_p):
        pl.semaphore_signal(barrier, inc=1, device_id=(to_s, to_p), device_id_type=MESH)

    def greet_seq(k, _):
        greet(lax.rem(s + k, NSEQ), p)
        return 0

    lax.fori_loop(1, NSEQ, greet_seq, 0)

    def greet_sources(k, _):
        greet(p * 8 + k // 3, lax.rem(p + 1 + lax.rem(k, 3), NSP))
        return 0

    lax.fori_loop(0, 24, greet_sources, 0)
    for ds in (-1, 0, 1):

        @pl.when(jnp.logical_and(s + ds >= 0, s + ds < NSEQ))
        def _():
            for dp in (1, 2, 3):
                greet(s + ds, lax.rem(p + dp, NSP))

    loads = []
    for c in range(CH):
        cols = pl.ds(c * CW, CW)
        kc = pltpu.make_async_copy(k_hbm.at[:, cols], k_s.at[c], ksem.at[c])
        vc = pltpu.make_async_copy(v_hbm.at[:, cols], v_s.at[c], vsem.at[c])
        kc.start()
        vc.start()
        loads.append((kc, vc))
    w_copy = pltpu.make_async_copy(w_hbm, w_s, wsem.at[0])
    head_rows = pl.ds(pl.multiple_of(p * FEAT, FEAT), FEAT)
    head_copy = pltpu.make_async_copy(headw_hbm.at[head_rows], headw_s, wsem.at[1])
    win_copy = pltpu.make_async_copy(win_hbm, win_s, wsem.at[2])
    wmid_copy = pltpu.make_async_copy(wmid_hbm, wmid_s, wsem.at[3])
    for copy in (win_copy, wmid_copy, w_copy, head_copy):
        copy.start()

    qs[...] = jnp.zeros(qs.shape, BF16)
    for c in range(CH):
        qs[c, 0:TOK, :] = q_ref[:, c * CW : (c + 1) * CW]
    q_own = pltpu.make_async_copy(qs, qg.at[:, s], lsem.at[0])
    q_own.start()

    ls[...] = jnp.zeros(ls.shape, F32)
    ls[:, 0:6, 0:16] = noisy_ref[...]
    ls[:, 0:6, 16:32] = platent_ref[0].astype(F32)
    ls[:, 0:6, 32:48] = platent_ref[1].astype(F32)
    fpad[...] = jnp.zeros(fpad.shape, F32)
    fpad[:, 0:6, :] = pfeat_ref[...].reshape(4, 6, VAE).astype(F32)
    fs[...] = fpad[...].reshape(32, VAE).astype(BF16)

    rows_in = 1 + jnp.where(s > 0, 1, 0) + jnp.where(s < NSEQ - 1, 1, 0)
    pl.semaphore_wait(barrier, NSEQ - 1 + jnp.where(owner_sp != p, NSEQ, 0) + 3 * rows_in)

    def send_chunk(buf, dst, c, send_sem, recv_sem, by_dest):
        def one(k, _):
            to = lax.rem(s + k, NSEQ)
            pltpu.make_async_remote_copy(
                src_ref=buf.at[c, to] if by_dest else buf.at[c],
                dst_ref=dst.at[c, s],
                send_sem=send_sem.at[c],
                recv_sem=recv_sem.at[c],
                device_id=(to, p),
                device_id_type=MESH,
            ).start()
            return 0

        lax.fori_loop(1, NSEQ, one, 0)

    for c in range(CH):
        send_chunk(qs, qg, c, q_send, q_recv, False)

    def near(fn):
        for ds in (-1, 0, 1):
            for dp in (-1, 0, 1):
                if ds == 0 and dp == 0:
                    continue
                inside_s = jnp.logical_and(s + ds >= 0, s + ds < NSEQ)
                inside_p = jnp.logical_and(p + dp >= 0, p + dp < NSP)
                pl.when(jnp.logical_and(inside_s, inside_p))(functools.partial(fn, ds, dp))

    def slot_of(ds, dp):
        return (ds + 1) * 3 + dp + 1

    def border_copies(ds, dp):
        out, back = slot_of(ds, dp), slot_of(-ds, -dp)
        return [
            pltpu.make_async_remote_copy(
                src_ref=src,
                dst_ref=dst.at[back],
                send_sem=send.at[out],
                recv_sem=recv.at[back],
                device_id=(s + ds, p + dp),
                device_id_type=MESH,
            )
            for src, dst, send, recv in ((ls, lr, l_send, l_recv), (fs, fr, f_send, f_recv))
        ]

    def border_start(ds, dp):
        for copy in border_copies(ds, dp):
            copy.start()

    def border_wait(ds, dp):
        slot = slot_of(ds, dp)
        wait_bytes(lr.at[slot], l_recv.at[slot])
        wait_bytes(fr.at[slot], f_recv.at[slot])
        wait_bytes(lr.at[slot], l_send.at[slot])
        wait_bytes(fr.at[slot], f_send.at[slot])

    near(border_start)

    visible = iota((1, HIST), 1) < valid_ref[0]
    ones = jnp.ones((HIST, HD), BF16)
    half = TOKENS // 2
    lane = iota((half, HD), 1) % 32
    q_own.wait()
    for c in range(CH):
        wait_bytes(qg.at[c, 0 : NSEQ - 1], q_recv.at[c])
        loads[c][0].wait()
        loads[c][1].wait()
        for r in range(2):
            first_owner = r * (NSEQ // 2)
            block = qg[c, first_owner : first_owner + NSEQ // 2]
            q = pack_rows(block.astype(F32)).astype(BF16)
            stats = jnp.zeros((half, HD), F32)
            for h in range(2):
                cols = slice(h * HD, (h + 1) * HD)
                scores = lax.dot_general(
                    q[:, cols],
                    k_s[c, :, cols],
                    (((1,), (1,)), ((), ())),
                    preferred_element_type=F32,
                )
                scores = jnp.where(visible, scores, -1e30)
                top = jnp.max(scores, axis=1, keepdims=True) * EXP2_SCALE
                top = top.astype(BF16).astype(F32)
                weights = jnp.exp2(scores * EXP2_SCALE - top).astype(BF16)
                both = jnp.concatenate([v_s[c, :, cols], ones], axis=1)
                acc = jnp.dot(weights, both, preferred_element_type=F32)
                total = acc[:, HD:]
                high = total.astype(BF16).astype(F32)
                stats = jnp.where(lane == h, top, stats)
                stats = jnp.where(lane == 2 + h, high, stats)
                stats = jnp.where(lane == 4 + h, total - high, stats)
                padded = pad_rows(acc[:, :HD])
                if h == 1:
                    st = pad_rows(stats)
                    at = iota(st.shape, 2)
                    spare = jnp.where(
                        at < 32,
                        pltpu.roll(st, 12, 1),
                        jnp.where(at < 64, pltpu.roll(st, 8, 1), pltpu.roll(st, 4, 1)),
                    )
                    padded = jnp.where(iota(st.shape, 1) < TOK, padded, spare)
                pc[c, first_owner : first_owner + NSEQ // 2, :, cols] = padded.astype(BF16)
        own = pltpu.make_async_copy(pc.at[c, s], rc.at[c, s], lsem.at[1 + c])
        own.start()
        send_chunk(pc, rc, c, c_send, c_recv, True)

    near(border_wait)
    win_copy.wait()
    wmid_copy.wait()
    lr[4] = ls[...]
    fr[4] = fs[...]
    cells[...] = jnp.zeros(cells.shape, F32)
    feats[...] = jnp.zeros(feats.shape, F32)
    for ds in (-1, 0, 1):
        for dp in (-1, 0, 1):
            inside = jnp.logical_and(
                jnp.logical_and(s + ds >= 0, s + ds < NSEQ),
                jnp.logical_and(p + dp >= 0, p + dp < NSP),
            )
            slot = slot_of(ds, dp)
            src = {-1: slice(4, 6), 0: slice(0, 6), 1: slice(0, 2)}[dp]
            dst = {-1: slice(0, 2), 0: slice(2, 8), 1: slice(8, 10)}[dp]
            for g in range(3):
                part = lr[slot, :, src, g * 16 : (g + 1) * 16]
                cells[g, 2 * ds + 2 : 2 * ds + 4, dst, :] = jnp.where(inside, part, 0.0)
            src = {-1: slice(5, 6), 0: slice(0, 6), 1: slice(0, 1)}[dp]
            dst = {-1: slice(0, 1), 0: slice(1, 7), 1: slice(7, 8)}[dp]
            part = fr[slot].astype(F32).reshape(2, 2, 8, VAE)
            part = jnp.where(inside, part, 0.0)
            rows = {-1: (1,), 0: (0, 1), 1: (0,)}[ds]
            for row in rows:
                for f in range(2):
                    feats[f, {-1: 0, 0: 1 + row, 1: 3}[ds], dst, :] = part[f, row, src, :]

    def window(ref, g, dy, dx, height):
        return ref[g, dy : dy + height, dx : dx + 8, :].reshape(height * 8, -1).astype(BF16)

    def taps():
        return [(dy, dx) for dy in range(3) for dx in range(3)]

    first = jnp.zeros((32, VAE), F32) + bias_ref[0:1, :]
    mid = jnp.zeros((16, VAE), F32) + bias_ref[2:3, :]
    for f in range(2):
        for dy, dx in taps():
            tap = f * 9 + dy * 3 + dx
            first += jnp.dot(window(cells, f + 1, dy, dx, 4), win_s[tap], preferred_element_type=F32)
            mid += jnp.dot(window(feats, f, dy, dx, 2), wmid_s[tap], preferred_element_type=F32)
    firsts[:, 0:8, :] = first.reshape(4, 8, VAE)

    row = iota((PAD, HD), 0)
    for c in range(CH):
        pltpu.make_async_copy(pc.at[c, s], rc.at[c, s], lsem.at[1 + c]).wait()
        wait_bytes(rc.at[c, 0 : NSEQ - 1], c_recv.at[c])
        tile = rc[c, :, :, HD : 2 * HD].astype(F32)
        at = iota(tile.shape, 1)
        st = jnp.where(
            at < 4,
            pltpu.roll(tile, 4, 1),
            jnp.where(
                at < 8,
                pltpu.roll(pltpu.roll(tile, HD - 32, 2), 8, 1),
                pltpu.roll(pltpu.roll(tile, HD - 64, 2), 12, 1),
            ),
        )
        top = jnp.max(st, axis=0, keepdims=True)
        factor = jnp.exp2(st - top)
        sums = pltpu.roll(st, HD - 2, 2) + pltpu.roll(st, HD - 4, 2)
        total = jnp.sum(factor * sums, axis=0, keepdims=True)
        factor = factor / total
        for h in range(2):
            part = rc[c, :, :, h * HD : (h + 1) * HD].astype(F32)
            merged = jnp.sum(part * factor[:, :, h : h + 1], axis=0)
            merged = jnp.where(row < TOK, merged, 0.0)
            ao[c, :, h * HD : (h + 1) * HD] = merged.astype(BF16)
        own = pltpu.make_async_copy(ao.at[c], ag.at[c, s], lsem.at[1 + CH + c])
        own.start()
        send_chunk(ao, ag, c, d_send, d_recv, False)

    w_copy.wait()
    result = jnp.zeros((NSEQ * PAD, COLS), F32)
    for c in range(CH):
        pltpu.make_async_copy(ao.at[c], ag.at[c, s], lsem.at[1 + CH + c]).wait()
        wait_bytes(ag.at[c, 0 : NSEQ - 1], d_recv.at[c])
        block = ag[c].reshape(NSEQ * PAD, CW)
        result += jnp.dot(block, w_s[c * CW : (c + 1) * CW, :], preferred_element_type=F32)
    es[:, :, 0:COLS] = result.reshape(NSEQ, PAD, COLS).astype(BF16)
    es[:, :, COLS:] = jnp.zeros((NSEQ, PAD, 256 - COLS), BF16)
    e_slot = piece * NSP + p
    same = owner_sp == p

    def send_piece(k, _):
        to = lax.rem(s + k, NSEQ)
        pltpu.make_async_remote_copy(
            src_ref=es.at[to],
            dst_ref=er.at[e_slot],
            send_sem=e_send,
            recv_sem=e_recv,
            device_id=(to, owner_sp),
            device_id_type=MESH,
        ).start()
        return 0

    lax.fori_loop(1, NSEQ, send_piece, 0)

    @pl.when(same)
    def _():
        own = pltpu.make_async_copy(es.at[s], er.at[e_slot], lsem.at[1 + 2 * CH])
        own.start()
        own.wait()
        wait_bytes(er.at[0 : NSEQ - 1], e_recv)

    @pl.when(jnp.logical_not(same))
    def _():
        send_piece(0, 0)
        wait_bytes(er, e_recv)

    for j in range(8):
        part = er[j * NSP : (j + 1) * NSP].astype(F32)
        proj[:, j * COLS : (j + 1) * COLS] = jnp.sum(part, axis=0)[:, 0:COLS]
    upd[...] = jnp.zeros(upd.shape, F32)
    upd[0:TOK, :] = hidden_ref[...].astype(F32)
    updated = upd[...] + rows_ref[0:1, :] * proj[...]
    hidden_out[...] = updated[0:TOK].astype(BF16)
    gain, shift = rows_ref[1:2, :], rows_ref[2:3, :]
    at = iota((PAD, FEAT), 0)
    left = jnp.where(at < TOK, updated * gain, jnp.where(at == TOK, gain, shift))
    head_copy.wait()
    part = jnp.dot(
        left, headw_s[...], precision=lax.Precision.HIGHEST, preferred_element_type=F32
    )
    gs[...] = jnp.zeros(gs.shape, F32)
    gs[:, 0:64] = part
    gs[:, 64:65] = jnp.sum(updated, axis=1, keepdims=True)
    gs[:, 65:66] = jnp.sum(updated * updated, axis=1, keepdims=True)

    def share(fn):
        for ds in (-1, 0, 1):
            for dp in range(NSP):
                if ds == 0 and dp == 0:
                    continue
                inside = jnp.logical_and(s + ds >= 0, s + ds < NSEQ)
                pl.when(inside)(functools.partial(fn, ds, dp))

    def g_start(ds, dp):
        pltpu.make_async_remote_copy(
            src_ref=gs,
            dst_ref=gr.at[(1 - ds) * NSP + dp],
            send_sem=g_send.at[(ds + 1) * NSP + dp],
            recv_sem=g_recv.at[(1 - ds) * NSP + dp],
            device_id=(s + ds, lax.rem(p + dp, NSP)),
            device_id_type=MESH,
        ).start()

    def g_wait(ds, dp):
        slot = (ds + 1) * NSP + dp
        wait_bytes(gr.at[slot], g_recv.at[slot])
        wait_bytes(gr.at[slot], g_send.at[slot])

    share(g_start)
    gr[NSP] = gs[...]
    share(g_wait)

    vtok[...] = jnp.zeros(vtok.shape, F32)
    vcell[...] = jnp.zeros(vcell.shape, F32)
    for ds in (-1, 0, 1):
        inside = jnp.logical_and(s + ds >= 0, s + ds < NSEQ)
        total = gr[(ds + 1) * NSP]
        for dp in range(1, NSP):
            total = total + gr[(ds + 1) * NSP + dp]
        mean = total[0:TOK, 64:65] / D
        var = total[0:TOK, 65:66] / D - mean * mean
        scaled = (total[0:TOK, 0:64] - mean * total[12:13, 0:64]) * lax.rsqrt(var + 1e-6)
        velocity = scaled + total[13:14, 0:64] + vecs_ref[0:1, 0:64]
        vtok[ds + 1, 1 : TOK + 1, 0:64] = jnp.where(inside, velocity, 0.0)
        around = vtok[ds + 1, pl.ds(3 * p, 8), :]
        for a in range(2):
            for c2 in range(2):
                col = (a * 2 + c2) * 16
                vcell[2 * ds + 2 + a, pl.ds(c2, 8, stride=2), :] = around[:, col : col + 16]

    clean = cells[0] - NOISE * vcell[...]
    cells[0] = clean
    first = firsts[:, 0:8, :].reshape(32, VAE)
    for dy, dx in taps():
        first += jnp.dot(
            window(cells, 0, dy, dx, 4), win_s[18 + dy * 3 + dx], preferred_element_type=F32
        )
    norm = lax.rsqrt(jnp.mean(first * first, axis=-1, keepdims=True) + 1e-6)
    z = first * norm * bias_ref[1:2, :]
    act = z / (1.0 + jnp.exp(-z))
    pos = iota((32, VAE), 0)
    y = 2 * s - 1 + pos // 8
    x = 6 * p - 1 + pos % 8
    inside = (y >= 0) & (y < 2 * NSEQ) & (x >= 0) & (x < 24)
    act = jnp.where(inside, act, 0.0)
    firsts[:, 0:8, :] = first.reshape(4, 8, VAE)
    acts[...] = jnp.zeros(acts.shape, F32)
    acts[0, :, 0:8, :] = act.reshape(4, 8, VAE)
    out = mid + firsts[1:3, 1:9, :].reshape(16, VAE)
    for dy, dx in taps():
        out += jnp.dot(
            window(acts, 0, dy, dx, 2), wmid_s[18 + dy * 3 + dx], preferred_element_type=F32
        )
    decoded_out[...] = out.reshape(2, 8, VAE)[:, 0:6, :]

    for c in range(CH):
        wait_bytes(qg.at[c, 0 : NSEQ - 1], q_send.at[c])
        wait_bytes(qg.at[c, 0 : NSEQ - 1], c_send.at[c])
        wait_bytes(qg.at[c, 0 : NSEQ - 1], d_send.at[c])

    @pl.when(same)
    def _():
        wait_bytes(er.at[0 : NSEQ - 1], e_send)

    @pl.when(jnp.logical_not(same))
    def _():
        wait_bytes(er, e_send)


def local(
    group_hidden,
    queries,
    history_keys,
    history_values,
    valid_len,
    out_weight,
    attn_gate,
    head_gain,
    head_shift,
    head_weight,
    head_bias,
    noisy_latent,
    prev_latent,
    prev_feat,
    conv_in_weight,
    conv_in_bias,
    vae_gain,
    conv_mid_weight,
    conv_mid_bias,
):
    start = lax.axis_index("sp") * FEAT
    gain = lax.dynamic_slice_in_dim(head_gain, start, FEAT, 0)
    shift = lax.dynamic_slice_in_dim(head_shift, start, FEAT, 0)
    zero = jnp.zeros_like(attn_gate)
    rows = jnp.stack([attn_gate, gain, shift] + [zero] * 5)
    none = jnp.zeros_like(vae_gain)
    biases = jnp.stack([conv_in_bias, vae_gain, conv_mid_bias] + [none] * 5)
    vecs = jnp.pad(head_bias[None], ((0, 7), (0, 64)))
    vmem = pl.BlockSpec(memory_space=pltpu.VMEM)
    hbm = pl.BlockSpec(memory_space=pl.ANY)
    smem = pl.BlockSpec(memory_space=pltpu.SMEM)
    blocks = (CH, NSEQ, PAD, CW)
    dma = pltpu.SemaphoreType.DMA
    return pl.pallas_call(
        kernel,
        out_shape=(
            jax.ShapeDtypeStruct((TOK, FEAT), BF16),
            jax.ShapeDtypeStruct((2, 6, VAE), F32),
        ),
        in_specs=[vmem, vmem, hbm, hbm, smem, hbm, vmem, vmem, vmem, hbm, vmem, vmem, vmem, hbm, hbm],
        out_specs=(vmem, vmem),
        scratch_shapes=[
            pltpu.VMEM((CH, HIST, CW), BF16),
            pltpu.VMEM((CH, HIST, CW), BF16),
            pltpu.VMEM((FEAT, COLS), BF16),
            pltpu.VMEM((FEAT, 64), F32),
            pltpu.VMEM((27, 16, VAE), BF16),
            pltpu.VMEM((27, VAE, VAE), BF16),
            pltpu.VMEM((CH, PAD, CW), BF16),
            pltpu.VMEM(blocks, BF16),
            pltpu.VMEM(blocks, BF16),
            pltpu.VMEM(blocks, BF16),
            pltpu.VMEM((CH, PAD, CW), BF16),
            pltpu.VMEM(blocks, BF16),
            pltpu.VMEM((NSEQ, PAD, 256), BF16),
            pltpu.VMEM((NSEQ, PAD, 256), BF16),
            pltpu.VMEM((PAD, HD), F32),
            pltpu.VMEM((3 * NSP, PAD, HD), F32),
            pltpu.VMEM((2, 8, HD), F32),
            pltpu.VMEM((9, 2, 8, HD), F32),
            pltpu.VMEM((32, VAE), BF16),
            pltpu.VMEM((9, 32, VAE), BF16),
            pltpu.VMEM((4, 8, VAE), F32),
            pltpu.VMEM((3, 6, 16, 16), F32),
            pltpu.VMEM((3, 24, HD), F32),
            pltpu.VMEM((6, 16, 16), F32),
            pltpu.VMEM((2, 4, 16, VAE), F32),
            pltpu.VMEM((4, 16, VAE), F32),
            pltpu.VMEM((1, 4, 16, VAE), F32),
            pltpu.VMEM((PAD, FEAT), F32),
            pltpu.VMEM((PAD, FEAT), F32),
            dma((CH,)),
            dma((CH,)),
            dma((4,)),
            dma((2 + 2 * CH,)),
            dma((CH,)),
            dma((CH,)),
            dma((CH,)),
            dma((CH,)),
            dma((CH,)),
            dma((CH,)),
            dma,
            dma,
            dma((3 * NSP,)),
            dma((3 * NSP,)),
            dma((9,)),
            dma((9,)),
            dma((9,)),
            dma((9,)),
        ],
        compiler_params=pltpu.CompilerParams(
            collective_id=0, has_side_effects=True, vmem_limit_bytes=56 << 20
        ),
    )(
        group_hidden,
        queries,
        history_keys,
        history_values,
        valid_len,
        out_weight,
        rows,
        vecs,
        biases,
        head_weight,
        noisy_latent,
        prev_latent,
        prev_feat,
        conv_in_weight.reshape(27, 16, VAE),
        conv_mid_weight.reshape(27, VAE, VAE),
    )


def solution(mesh):
    placed = (
        P("seq", "sp"),
        P("seq", "sp"),
        P("seq", "sp"),
        P("seq", "sp"),
        P("seq"),
        P("sp", "seq"),
        P("sp"),
        P(),
        P(),
        P(),
        P(),
        P("seq", "sp", None),
        P(None, "seq", "sp", None),
        P(None, "seq", "sp", None),
        P(),
        P(),
        P(),
        P(),
        P(),
    )
    return jax.shard_map(
        local,
        mesh=mesh,
        in_specs=placed,
        out_specs=(P("seq", "sp"), P("seq", "sp", None)),
        check_vma=False,
    )
```

time: 1060 us -> 103 us (0.10)
  waiting for transfers between devices: 340 us -> 0 us
  blocking collectives: 270 us -> 0 us
  local copies, waits for them, and re-layouts: 240 us -> 18.6 us
  other arithmetic: 115 us -> 0 us
  Pallas kernels: 0 us -> 82.1 us
  matrix products: 42.2 us -> 0 us
  starting transfers between devices: 32 us -> 0 us
  between operations: 15.9 us -> 1.3 us
    all_gather x1 -> x0, waiting for transfers between devices: 318 us -> none  [joined(): pieces = jax.tree.map(lambda part: lax.all_gather(part, axis), value)]
    all_gather x3 -> x0, blocking collectives: 243 us -> none  [the longest x2 165 us: joined(): pieces = jax.tree.map(lambda part: lax.all_gather(part, axis), value)]
    dynamic_slice x95 -> x2, local copies, waits for them, and re-layouts: 183 us -> 1.56 us  [the longest x1 0.78 us: local(): shift = lax.dynamic_slice_in_dim(head_shift, start, FEAT, 0)]
    add x62 -> x0, other arithmetic: 96.2 us -> none  [the longest x31 95.3 us: join_partials(): accum = accum_a * widen(scale_a, HD) + accum_b * widen(scale_b, HD)]
    pallas_call x0 -> x1, Pallas kernels: none -> 82.1 us  [local(): pl.pallas_call(kernel, out_shape=(jax.ShapeDtypeStruct((TOK, FEAT), BF16)...]
    slice x70 -> x0, local copies, waits for them, and re-layouts: 44.4 us -> none  [the longest x5 42.4 us: joined(): tail = jax.tree.map(lambda part: part[1:], pieces)]
    dot_general x24 -> x0, matrix products: 42.2 us -> none  [the longest x10 17.9 us: one_head(): lax.dot_general(query_head, key_head, (((1,), (1,)), ((), ())), preferred...]
    ppermute x8 -> x0, starting transfers between devices: 31.9 us -> none  [the longest x4 16.8 us: with_halo(): before = lax.ppermute(last, axis, up)]
  transfers between devices with their start and end apart: 10 -> 0, of which waited for: 6 -> 0; matrix products, arithmetic and copies ran while one was open for 0% -> 0% of each run, Pallas kernels for 0% -> 0%
where the time goes in v1:
time: 103 us; the launch traced here: 102 us
  Pallas kernels  82.1 us (80%)
  local copies, waits for them, and re-layouts  18.6 us (18%)
  between operations  1.3 us (1%)
    pallas_call x1, Pallas kernels, local(): pl.pallas_call(kernel, out_shape=(jax.ShapeDtypeStruct((TOK, FEAT), BF16)...  82.1 us
    unnamed x6, local copies, waits for them, and re-layouts  10.4 us
    another operation x6, local copies, waits for them, and re-layouts, local(): biases = jnp.stack([conv_in_bias, vae_gain, conv_mid_bias] + [none] * 5)  2.67 us

profile of v1, /device:TPU:3, one launch (start us, length us, event | category | flops | bytes accessed | tf_op | source)
XLA Modules:
  0.0 102.0 jit_solution(2046001608572059453)
XLA Ops:
  1.3 0.7 stack.35
  2.0 0.7 stack.36
  2.6 0.7 stack.37
  3.3 1.3 %pad.4.vecs_ref = f32[8,128]{1,0:T(8,128)} pad(f32[1,64]{1,0:T(1,128)} %bitcast.5, f32[]{:T(128)} %constant.2.clone.1), padding=0_7x0_64 | pad | bytes 4356 | tf_op jit(solution)/shard_map/jit(_pad)/pad | solution.py:531
  4.6 0.7 stack.30
  5.3 0.6 stack.39.bias_ref
  5.9 0.8 dynamic_slice.6
  6.7 0.8 dynamic_slice.7
  7.5 1.3 %copy.23.noisy_ref = f32[2,6,16]{2,1,0:T(8,128)} copy(f32[2,6,16]{2,0,1:T(2,128)} %param.30) | data formatting | bytes 1536 | tf_op args[11]
  8.8 1.3 %copy.24.platent_ref = bf16[2,2,6,16]{3,2,1,0:T(8,128)(2,1)} copy(bf16[2,2,6,16]{3,1,2,0:T(2,128)(2,1)} %param.31) | data formatting | bytes 1536 | tf_op args[12]
  10.1 0.7 stack.34.rows_ref
  10.7 1.3 %copy.25.pfeat_ref = bf16[2,2,6,384]{3,2,1,0:T(8,128)(2,1)} copy(bf16[2,2,6,384]{3,1,2,0:T(2,128)(2,1)} %param.32) | data formatting | bytes 36864 | tf_op args[13]
  12.1 2.1 %copy.21.w_hbm = bf16[1280,160]{1,0:T(8,128)(2,1)} copy(bf16[1280,160]{0,1:T(8,128)(2,1)} %param.24) | data formatting | bytes 819200 | tf_op args[5]
  14.1 3.0 %copy.22.headw_hbm = f32[5120,64]{1,0:T(8,128)} copy(f32[5120,64]{0,1:T(8,128)} %param.28) | data formatting | bytes 2621440 | tf_op args[9]
  17.2 82.1 %shard_map.194 = (bf16[12,1280]{1,0:T(8,128)(2,1)}, f32[2,6,384]{2,1,0:T(8,128)}) custom-call(bf16[12,1280]{1,0:T(8,128)(2,1)} %hidden_ref.1, bf16[12,1280]{1,0:T(8,128)(2,1)} %q_ref.1, bf16[2048,1280]{1,0:T(8,128)(2,1)} %k_hbm.1, bf16[2048,1280]{1,0:T(8,128)(2,1)} %v_hbm.1, s32[1]{0:T(128)S(6)} %copy.28.valid_ref, bf16[1280,160]{1,0:T(8,128)(2,1)} %copy.21.w_hbm, ...), custom_call_target="tpu_custom_call" | custom-call | tf_op jit(solution)/shard_map/pallas_call | solution.py:537
  99.3 1.4 %copy.26 = f32[2,6,384]{2,0,1:T(2,128)} copy(f32[2,6,384]{2,1,0:T(8,128)} %get-tuple-element.3) | data formatting | bytes 36864 | tf_op jit(solution)/shard_map/pallas_call | solution.py:537
  100.6 1.4 %copy.29 = bf16[12,1280]{1,0:T(8,128)(2,1)} copy(bf16[12,1280]{1,0:T(8,128)(2,1)} %get-tuple-element.6) | data formatting | bytes 61440
  (6 shorter events, 0.0 us)

commit v2 on v1

--- a/solution.py
+++ b/solution.py
@@ -24,6 +24,11 @@
 COLS = 160
 CH = 5
 CW = FEAT // CH
+LINE = 4
+PLANE = NSEQ // LINE
+ROWS = PLANE * TOK
+BY_Y = (False, True, False, True, False)
+LAST = CH - 1
 VAE = 384
 EXP2_SCALE = math.log2(math.e) / math.sqrt(HD)
 NOISE = 0.75
@@ -31,6 +36,10 @@
 
 def iota(shape, dim):
     return lax.broadcasted_iota(jnp.int32, shape, dim)
+
+
+def row_of(ref, start, count):
+    return jnp.concatenate([ref[pl.ds(start + k, 1), :] for k in range(count)], axis=1)
 
 
 def wait_bytes(region, sem):
@@ -62,9 +71,13 @@
     v_hbm,
     valid_ref,
     w_hbm,
-    rows_ref,
-    vecs_ref,
-    bias_ref,
+    gate_ref,
+    gain_ref,
+    shift_ref,
+    headb_ref,
+    bias_in_ref,
+    vgain_ref,
+    bias_mid_ref,
     headw_hbm,
     noisy_ref,
     platent_ref,
@@ -77,13 +90,18 @@
     v_s,
     w_s,
     headw_s,
+    headg_s,
     win_s,
     wmid_s,
     qs,
-    qg,
+    qd,
+    qp,
+    ql,
+    ao,
+    agp,
+    agl,
     pc,
     rc,
-    ao,
     ag,
     es,
     er,
@@ -106,12 +124,16 @@
     vsem,
     wsem,
     lsem,
-    q_send,
-    q_recv,
+    q1_send,
+    q1_recv,
+    q2_send,
+    q2_recv,
+    d1_send,
+    d1_recv,
+    d2_send,
+    d2_recv,
     c_send,
     c_recv,
-    d_send,
-    d_recv,
     e_send,
     e_recv,
     g_send,
@@ -158,8 +180,8 @@
         vc.start()
         loads.append((kc, vc))
     w_copy = pltpu.make_async_copy(w_hbm, w_s, wsem.at[0])
-    head_rows = pl.ds(pl.multiple_of(p * FEAT, FEAT), FEAT)
-    head_copy = pltpu.make_async_copy(headw_hbm.at[head_rows], headw_s, wsem.at[1])
+    head_cols = pl.ds(pl.multiple_of(p * FEAT, FEAT), FEAT)
+    head_copy = pltpu.make_async_copy(headw_hbm.at[:, head_cols], headw_s, wsem.at[1])
     win_copy = pltpu.make_async_copy(win_hbm, win_s, wsem.at[2])
     wmid_copy = pltpu.make_async_copy(wmid_hbm, wmid_s, wsem.at[3])
     for copy in (win_copy, wmid_copy, w_copy, head_copy):
@@ -168,28 +190,78 @@
     qs[...] = jnp.zeros(qs.shape, BF16)
     for c in range(CH):
         qs[c, 0:TOK, :] = q_ref[:, c * CW : (c + 1) * CW]
-    q_own = pltpu.make_async_copy(qs, qg.at[:, s], lsem.at[0])
-    q_own.start()
+    x_at, y_at, z_at = s // 8, lax.rem(s // 2, 4), lax.rem(s, 2)
+
+    def line_at(c):
+        return y_at if BY_Y[c] else x_at
+
+    def plane_at(c):
+        return x_at * 2 + z_at if BY_Y[c] else y_at * 2 + z_at
+
+    def line_peer(c, line):
+        return x_at * 8 + line * 2 + z_at if BY_Y[c] else line * 8 + y_at * 2 + z_at
+
+    def plane_peer(c, at):
+        return (at // 2) * 8 + y_at * 2 + lax.rem(at, 2) if BY_Y[c] else x_at * 8 + at
+
+    def to_line(c, buf, dst, send_sem, recv_sem, by_dest):
+        for k in range(1, LINE):
+            line = lax.rem(line_at(c) + k, LINE)
+            pltpu.make_async_remote_copy(
+                src_ref=buf.at[c, line if by_dest else line_at(c)],
+                dst_ref=dst.at[c, line_at(c)],
+                send_sem=send_sem.at[c],
+                recv_sem=recv_sem.at[c],
+                device_id=(line_peer(c, line), p),
+                device_id_type=MESH,
+            ).start()
+
+    def to_plane(c, buf, dst, send_sem, recv_sem, by_dest):
+        for k in range(1, PLANE):
+            at = lax.rem(plane_at(c) + k, PLANE)
+            pltpu.make_async_remote_copy(
+                src_ref=buf.at[c, at] if by_dest else buf.at[c],
+                dst_ref=dst.at[c, plane_at(c)],
+                send_sem=send_sem.at[c],
+                recv_sem=recv_sem.at[c],
+                device_id=(plane_peer(c, at), p),
+                device_id_type=MESH,
+            ).start()
+
+    def wait_line(c, dst, sem):
+        wait_bytes(dst.at[c, 0 : LINE - 1], sem.at[c])
+
+    def wait_plane(c, dst, sem):
+        wait_bytes(dst.at[c, 0 : PLANE - 1], sem.at[c])
 
     ls[...] = jnp.zeros(ls.shape, F32)
-    ls[:, 0:6, 0:16] = noisy_ref[...]
-    ls[:, 0:6, 16:32] = platent_ref[0].astype(F32)
-    ls[:, 0:6, 32:48] = platent_ref[1].astype(F32)
+    for x in range(6):
+        ls[:, x, 0:16] = noisy_ref[x]
+        ls[:, x, 16:32] = platent_ref[0, x].astype(F32)
+        ls[:, x, 32:48] = platent_ref[1, x].astype(F32)
     fpad[...] = jnp.zeros(fpad.shape, F32)
-    fpad[:, 0:6, :] = pfeat_ref[...].reshape(4, 6, VAE).astype(F32)
-    fs[...] = fpad[...].reshape(32, VAE).astype(BF16)
+    for f in range(2):
+        for x in range(6):
+            for r in range(2):
+                fpad[2 * r + f, x, :] = pfeat_ref[f, x, r].astype(F32)
+    fs[...] = fpad[...].reshape(2, 2 * 8, VAE).astype(BF16)
 
     rows_in = 1 + jnp.where(s > 0, 1, 0) + jnp.where(s < NSEQ - 1, 1, 0)
     pl.semaphore_wait(barrier, NSEQ - 1 + jnp.where(owner_sp != p, NSEQ, 0) + 3 * rows_in)
 
-    def send_chunk(buf, dst, c, send_sem, recv_sem, by_dest):
+    def place(c, owner):
+        if not BY_Y[c]:
+            return owner
+        return lax.rem(owner // 2, 4) * 8 + (owner // 8) * 2 + lax.rem(owner, 2)
+
+    def to_all(src, dst, send_sem, recv_sem):
         def one(k, _):
             to = lax.rem(s + k, NSEQ)
             pltpu.make_async_remote_copy(
-                src_ref=buf.at[c, to] if by_dest else buf.at[c],
-                dst_ref=dst.at[c, s],
-                send_sem=send_sem.at[c],
-                recv_sem=recv_sem.at[c],
+                src_ref=src(to),
+                dst_ref=dst,
+                send_sem=send_sem,
+                recv_sem=recv_sem,
                 device_id=(to, p),
                 device_id_type=MESH,
             ).start()
@@ -197,8 +269,13 @@
 
         lax.fori_loop(1, NSEQ, one, 0)
 
-    for c in range(CH):
-        send_chunk(qs, qg, c, q_send, q_recv, False)
+    def wait_all(dst, sem):
+        wait_bytes(dst.at[0 : NSEQ - 1], sem)
+
+    to_all(lambda to: qs.at[0], qd.at[s], q2_send.at[0], q2_recv.at[0])
+    for c in range(1, CH):
+        to_plane(c, qs, qp, q1_send, q1_recv, False)
+    qd[pl.ds(s, 1)] = qs[0][None]
 
     def near(fn):
         for ds in (-1, 0, 1):
@@ -214,16 +291,20 @@
 
     def border_copies(ds, dp):
         out, back = slot_of(ds, dp), slot_of(-ds, -dp)
+        rows = {-1: slice(0, 1), 0: slice(0, 2), 1: slice(1, 2)}[ds]
         return [
             pltpu.make_async_remote_copy(
                 src_ref=src,
-                dst_ref=dst.at[back],
+                dst_ref=dst,
                 send_sem=send.at[out],
                 recv_sem=recv.at[back],
                 device_id=(s + ds, p + dp),
                 device_id_type=MESH,
             )
-            for src, dst, send, recv in ((ls, lr, l_send, l_recv), (fs, fr, f_send, f_recv))
+            for src, dst, send, recv in (
+                (ls, lr.at[back], l_send, l_recv),
+                (fs.at[rows], fr.at[back, rows], f_send, f_recv),
+            )
         ]
 
     def border_start(ds, dp):
@@ -232,34 +313,65 @@
 
     def border_wait(ds, dp):
         slot = slot_of(ds, dp)
+        part = fr.at[slot, 0:1] if ds else fr.at[slot]
         wait_bytes(lr.at[slot], l_recv.at[slot])
-        wait_bytes(fr.at[slot], f_recv.at[slot])
+        wait_bytes(part, f_recv.at[slot])
         wait_bytes(lr.at[slot], l_send.at[slot])
-        wait_bytes(fr.at[slot], f_send.at[slot])
-
-    near(border_start)
+        wait_bytes(part, f_send.at[slot])
+
 
     visible = iota((1, HIST), 1) < valid_ref[0]
     ones = jnp.ones((HIST, HD), BF16)
     half = TOKENS // 2
     lane = iota((half, HD), 1) % 32
-    q_own.wait()
-    for c in range(CH):
-        wait_bytes(qg.at[c, 0 : NSEQ - 1], q_recv.at[c])
+    across = (((1,), (1,)), ((), ()))
+
+    def spread_queries(c):
+        qp[c, pl.ds(plane_at(c), 1)] = qs[c][None]
+        wait_plane(c, qp, q1_recv)
+        ql[c, pl.ds(line_at(c), 1)] = pack_rows(qp[c].astype(F32)).astype(BF16)[None]
+        to_line(c, ql, ql, q2_send, q2_recv, False)
+
+    def attend_ready(c):
+        if c == 0:
+            wait_all(qd, q2_recv.at[0])
+        else:
+            wait_line(c, ql, q2_recv)
         loads[c][0].wait()
         loads[c][1].wait()
+
+    def spare_rows(st):
+        at = iota(st.shape, 2)
+        return jnp.where(
+            at < 32,
+            pltpu.roll(st, 12, 1),
+            jnp.where(at < 64, pltpu.roll(st, 8, 1), pltpu.roll(st, 4, 1)),
+        )
+
+    def tokens_of(tile):
+        at = iota(tile.shape, 1)
+        return jnp.where(
+            at < 4,
+            pltpu.roll(tile, 4, 1),
+            jnp.where(
+                at < 8,
+                pltpu.roll(pltpu.roll(tile, HD - 32, 2), 8, 1),
+                pltpu.roll(pltpu.roll(tile, HD - 64, 2), 12, 1),
+            ),
+        )
+
+    def attend(c):
         for r in range(2):
-            first_owner = r * (NSEQ // 2)
-            block = qg[c, first_owner : first_owner + NSEQ // 2]
-            q = pack_rows(block.astype(F32)).astype(BF16)
+            owners = slice(r * (NSEQ // 2), (r + 1) * (NSEQ // 2))
+            if c == 0:
+                q = pack_rows(qd[owners].astype(F32)).astype(BF16)
+            else:
+                q = ql[c, 2 * r : 2 * r + 2].reshape(half, CW)
             stats = jnp.zeros((half, HD), F32)
             for h in range(2):
                 cols = slice(h * HD, (h + 1) * HD)
                 scores = lax.dot_general(
-                    q[:, cols],
-                    k_s[c, :, cols],
-                    (((1,), (1,)), ((), ())),
-                    preferred_element_type=F32,
+                    q[:, cols], k_s[c, :, cols], across, preferred_element_type=F32
                 )
                 scores = jnp.where(visible, scores, -1e30)
                 top = jnp.max(scores, axis=1, keepdims=True) * EXP2_SCALE
@@ -272,20 +384,64 @@
                 stats = jnp.where(lane == h, top, stats)
                 stats = jnp.where(lane == 2 + h, high, stats)
                 stats = jnp.where(lane == 4 + h, total - high, stats)
-                padded = pad_rows(acc[:, :HD])
+                tile = pad_rows(acc[:, :HD])
                 if h == 1:
-                    st = pad_rows(stats)
-                    at = iota(st.shape, 2)
-                    spare = jnp.where(
-                        at < 32,
-                        pltpu.roll(st, 12, 1),
-                        jnp.where(at < 64, pltpu.roll(st, 8, 1), pltpu.roll(st, 4, 1)),
-                    )
-                    padded = jnp.where(iota(st.shape, 1) < TOK, padded, spare)
-                pc[c, first_owner : first_owner + NSEQ // 2, :, cols] = padded.astype(BF16)
-        own = pltpu.make_async_copy(pc.at[c, s], rc.at[c, s], lsem.at[1 + c])
-        own.start()
-        send_chunk(pc, rc, c, c_send, c_recv, True)
+                    tile = jnp.where(iota(tile.shape, 1) < TOK, tile, spare_rows(pad_rows(stats)))
+                pc[c, owners, :, cols] = tile.astype(BF16)
+
+    def send_partials(c):
+        rc[c, pl.ds(s, 1)] = pc[c, pl.ds(place(c, s), 1)]
+        to_all(lambda to: pc.at[c, place(c, to)], rc.at[c, s], c_send.at[c], c_recv.at[c])
+
+    def merge_owned(c, parts):
+        st = tokens_of(parts[:, :, HD : 2 * HD].astype(F32))
+        top = jnp.max(st, axis=0, keepdims=True)
+        factor = jnp.exp2(st - top)
+        sums = pltpu.roll(st, HD - 2, 2) + pltpu.roll(st, HD - 4, 2)
+        factor = factor / jnp.sum(factor * sums, axis=0, keepdims=True)
+        row = iota((PAD, HD), 0)
+        for h in range(2):
+            part = parts[:, :, h * HD : (h + 1) * HD].astype(F32)
+            merged = jnp.sum(part * factor[:, :, h : h + 1], axis=0)
+            merged = jnp.where(row < TOK, merged, 0.0)
+            ao[c, :, h * HD : (h + 1) * HD] = merged.astype(BF16)
+
+    def spread_attention(c):
+        wait_plane(c, agp, d1_recv)
+        agl[c, pl.ds(line_at(c), 1)] = pack_rows(agp[c].astype(F32)).astype(BF16)[None]
+        to_line(c, agl, agl, d2_send, d2_recv, False)
+
+    def merge(c):
+        merge_owned(c, rc[c])
+        if c == LAST:
+            ag[pl.ds(s, 1)] = ao[c][None]
+        else:
+            agp[c, pl.ds(plane_at(c), 1)] = ao[c][None]
+
+    def send_attention(c):
+        if c == LAST:
+            to_all(lambda to: ao.at[c], ag.at[s], d2_send.at[c], d2_recv.at[c])
+        else:
+            to_plane(c, ao, agp, d1_send, d1_recv, False)
+
+    for c in range(1, CH):
+        spread_queries(c)
+    near(border_start)
+    for c in range(CH):
+        attend_ready(c)
+        if c >= 3:
+            wait_all(rc.at[c - 3], c_recv.at[c - 3])
+        attend(c)
+        if c >= 3:
+            merge(c - 3)
+        send_partials(c)
+        if c >= 3:
+            send_attention(c - 3)
+    for c in range(2, CH):
+        wait_all(rc.at[c], c_recv.at[c])
+        merge(c)
+        send_attention(c)
+        spread_attention(c - 2)
 
     near(border_wait)
     win_copy.wait()
@@ -313,7 +469,7 @@
             rows = {-1: (1,), 0: (0, 1), 1: (0,)}[ds]
             for row in rows:
                 for f in range(2):
-                    feats[f, {-1: 0, 0: 1 + row, 1: 3}[ds], dst, :] = part[f, row, src, :]
+                    feats[f, {-1: 0, 0: 1 + row, 1: 3}[ds], dst, :] = part[row, f, src, :]
 
     def window(ref, g, dy, dx, height):
         return ref[g, dy : dy + height, dx : dx + 8, :].reshape(height * 8, -1).astype(BF16)
@@ -321,8 +477,8 @@
     def taps():
         return [(dy, dx) for dy in range(3) for dx in range(3)]
 
-    first = jnp.zeros((32, VAE), F32) + bias_ref[0:1, :]
-    mid = jnp.zeros((16, VAE), F32) + bias_ref[2:3, :]
+    first = jnp.zeros((32, VAE), F32) + row_of(bias_in_ref, 0, 3)
+    mid = jnp.zeros((16, VAE), F32) + row_of(bias_mid_ref, 0, 3)
     for f in range(2):
         for dy, dx in taps():
             tap = f * 9 + dy * 3 + dx
@@ -330,44 +486,41 @@
             mid += jnp.dot(window(feats, f, dy, dx, 2), wmid_s[tap], preferred_element_type=F32)
     firsts[:, 0:8, :] = first.reshape(4, 8, VAE)
 
-    row = iota((PAD, HD), 0)
-    for c in range(CH):
-        pltpu.make_async_copy(pc.at[c, s], rc.at[c, s], lsem.at[1 + c]).wait()
-        wait_bytes(rc.at[c, 0 : NSEQ - 1], c_recv.at[c])
-        tile = rc[c, :, :, HD : 2 * HD].astype(F32)
-        at = iota(tile.shape, 1)
-        st = jnp.where(
-            at < 4,
-            pltpu.roll(tile, 4, 1),
-            jnp.where(
-                at < 8,
-                pltpu.roll(pltpu.roll(tile, HD - 32, 2), 8, 1),
-                pltpu.roll(pltpu.roll(tile, HD - 64, 2), 12, 1),
-            ),
-        )
-        top = jnp.max(st, axis=0, keepdims=True)
-        factor = jnp.exp2(st - top)
-        sums = pltpu.roll(st, HD - 2, 2) + pltpu.roll(st, HD - 4, 2)
-        total = jnp.sum(factor * sums, axis=0, keepdims=True)
-        factor = factor / total
-        for h in range(2):
-            part = rc[c, :, :, h * HD : (h + 1) * HD].astype(F32)
-            merged = jnp.sum(part * factor[:, :, h : h + 1], axis=0)
-            merged = jnp.where(row < TOK, merged, 0.0)
-            ao[c, :, h * HD : (h + 1) * HD] = merged.astype(BF16)
-        own = pltpu.make_async_copy(ao.at[c], ag.at[c, s], lsem.at[1 + CH + c])
-        own.start()
-        send_chunk(ao, ag, c, d_send, d_recv, False)
+    gate, gain = row_of(gate_ref, 0, 10), row_of(gain_ref, 10 * p, 10)
+    shift = row_of(shift_ref, 10 * p, 10)
+    head_copy.wait()
+    headg_s[...] = headw_s[...] * gain
+    fixed = lax.dot_general(
+        jnp.where(iota((PAD, FEAT), 0) == TOK, gain, shift),
+        headw_s[...],
+        across,
+        precision=lax.Precision.HIGHEST,
+        preferred_element_type=F32,
+    )
+    upd[...] = jnp.zeros(upd.shape, F32)
+    upd[0:TOK, :] = hidden_ref[...].astype(F32)
 
     w_copy.wait()
-    result = jnp.zeros((NSEQ * PAD, COLS), F32)
-    for c in range(CH):
-        pltpu.make_async_copy(ao.at[c], ag.at[c, s], lsem.at[1 + CH + c]).wait()
-        wait_bytes(ag.at[c, 0 : NSEQ - 1], d_recv.at[c])
-        block = ag[c].reshape(NSEQ * PAD, CW)
-        result += jnp.dot(block, w_s[c * CW : (c + 1) * CW, :], preferred_element_type=F32)
-    es[:, :, 0:COLS] = result.reshape(NSEQ, PAD, COLS).astype(BF16)
-    es[:, :, COLS:] = jnp.zeros((NSEQ, PAD, 256 - COLS), BF16)
+
+    def agl_ready(c):
+        wait_line(c, agl, d2_recv)
+        return agl[c].reshape(TOKENS, CW)
+
+    def project(c, block):
+        cols = w_s[:, c * CW : (c + 1) * CW]
+        return lax.dot_general(block, cols, across, preferred_element_type=F32)
+
+    by_x = pad_rows(project(0, agl_ready(0)) + project(2, agl_ready(2)))
+    by_y = project(1, agl_ready(1))
+    spread_attention(3)
+    by_y = pad_rows(by_y + project(3, agl_ready(3))).reshape(4, 4, 2, PAD, COLS)
+    result = by_x + jnp.stack([by_y[:, x] for x in range(4)]).reshape(NSEQ, PAD, COLS)
+    wait_all(ag, d2_recv.at[LAST])
+    result += project(LAST, ag[...].reshape(NSEQ * PAD, CW)).reshape(NSEQ, PAD, COLS)
+    rest = jnp.concatenate([result[:, :, HD:], jnp.zeros((NSEQ, PAD, 2 * HD - COLS), F32)], axis=2)
+    rest = rest + pltpu.roll(rest, 32, 2) + pltpu.roll(rest, 64, 2)
+    tile = jnp.where(iota(rest.shape, 1) < TOK, result[:, :, :HD], spare_rows(rest))
+    es[...] = tile.astype(BF16)
     e_slot = piece * NSP + p
     same = owner_sp == p
 
@@ -387,7 +540,7 @@
 
     @pl.when(same)
     def _():
-        own = pltpu.make_async_copy(es.at[s], er.at[e_slot], lsem.at[1 + 2 * CH])
+        own = pltpu.make_async_copy(es.at[s], er.at[e_slot], lsem.at[0])
         own.start()
         own.wait()
         wait_bytes(er.at[0 : NSEQ - 1], e_recv)
@@ -397,20 +550,21 @@
         send_piece(0, 0)
         wait_bytes(er, e_recv)
 
+    pieces = jnp.sum(er[...].astype(F32).reshape(8, NSP, PAD, HD), axis=1)
+    rests = tokens_of(pieces)
     for j in range(8):
-        part = er[j * NSP : (j + 1) * NSP].astype(F32)
-        proj[:, j * COLS : (j + 1) * COLS] = jnp.sum(part, axis=0)[:, 0:COLS]
-    upd[...] = jnp.zeros(upd.shape, F32)
-    upd[0:TOK, :] = hidden_ref[...].astype(F32)
-    updated = upd[...] + rows_ref[0:1, :] * proj[...]
+        proj[:, j * COLS : j * COLS + HD] = pieces[j]
+        proj[:, j * COLS + HD : (j + 1) * COLS] = rests[j, :, 0 : COLS - HD]
+    updated = jnp.where(iota((PAD, FEAT), 0) < TOK, upd[...] + gate * proj[...], 0.0)
     hidden_out[...] = updated[0:TOK].astype(BF16)
-    gain, shift = rows_ref[1:2, :], rows_ref[2:3, :]
-    at = iota((PAD, FEAT), 0)
-    left = jnp.where(at < TOK, updated * gain, jnp.where(at == TOK, gain, shift))
-    head_copy.wait()
-    part = jnp.dot(
-        left, headw_s[...], precision=lax.Precision.HIGHEST, preferred_element_type=F32
+    part = lax.dot_general(
+        updated,
+        headg_s[...],
+        across,
+        precision=lax.Precision.HIGHEST,
+        preferred_element_type=F32,
     )
+    part = jnp.where(iota((PAD, 64), 0) < TOK, part, fixed)
     gs[...] = jnp.zeros(gs.shape, F32)
     gs[:, 0:64] = part
     gs[:, 64:65] = jnp.sum(updated, axis=1, keepdims=True)
@@ -453,7 +607,7 @@
         mean = total[0:TOK, 64:65] / D
         var = total[0:TOK, 65:66] / D - mean * mean
         scaled = (total[0:TOK, 0:64] - mean * total[12:13, 0:64]) * lax.rsqrt(var + 1e-6)
-        velocity = scaled + total[13:14, 0:64] + vecs_ref[0:1, 0:64]
+        velocity = scaled + total[13:14, 0:64] + headb_ref[...]
         vtok[ds + 1, 1 : TOK + 1, 0:64] = jnp.where(inside, velocity, 0.0)
         around = vtok[ds + 1, pl.ds(3 * p, 8), :]
         for a in range(2):
@@ -469,7 +623,7 @@
             window(cells, 0, dy, dx, 4), win_s[18 + dy * 3 + dx], preferred_element_type=F32
         )
     norm = lax.rsqrt(jnp.mean(first * first, axis=-1, keepdims=True) + 1e-6)
-    z = first * norm * bias_ref[1:2, :]
+    z = first * norm * row_of(vgain_ref, 0, 3)
     act = z / (1.0 + jnp.exp(-z))
     pos = iota((32, VAE), 0)
     y = 2 * s - 1 + pos // 8
@@ -484,12 +638,20 @@
         out += jnp.dot(
             window(acts, 0, dy, dx, 2), wmid_s[18 + dy * 3 + dx], preferred_element_type=F32
         )
-    decoded_out[...] = out.reshape(2, 8, VAE)[:, 0:6, :]
-
+    out = out.reshape(2, 8, VAE)
+    for x in range(6):
+        decoded_out[x] = out[:, x, :]
+
+    wait_all(qd, q2_send.at[0])
     for c in range(CH):
-        wait_bytes(qg.at[c, 0 : NSEQ - 1], q_send.at[c])
-        wait_bytes(qg.at[c, 0 : NSEQ - 1], c_send.at[c])
-        wait_bytes(qg.at[c, 0 : NSEQ - 1], d_send.at[c])
+        wait_all(rc.at[c], c_send.at[c])
+        if c > 0:
+            wait_plane(c, qp, q1_send)
+            wait_line(c, ql, q2_send)
+        if c < LAST:
+            wait_plane(c, agp, d1_send)
+            wait_line(c, agl, d2_send)
+    wait_all(ag, d2_send.at[LAST])
 
     @pl.when(same)
     def _():
@@ -521,48 +683,44 @@
     conv_mid_weight,
     conv_mid_bias,
 ):
-    start = lax.axis_index("sp") * FEAT
-    gain = lax.dynamic_slice_in_dim(head_gain, start, FEAT, 0)
-    shift = lax.dynamic_slice_in_dim(head_shift, start, FEAT, 0)
-    zero = jnp.zeros_like(attn_gate)
-    rows = jnp.stack([attn_gate, gain, shift] + [zero] * 5)
-    none = jnp.zeros_like(vae_gain)
-    biases = jnp.stack([conv_in_bias, vae_gain, conv_mid_bias] + [none] * 5)
-    vecs = jnp.pad(head_bias[None], ((0, 7), (0, 64)))
     vmem = pl.BlockSpec(memory_space=pltpu.VMEM)
     hbm = pl.BlockSpec(memory_space=pl.ANY)
     smem = pl.BlockSpec(memory_space=pltpu.SMEM)
-    blocks = (CH, NSEQ, PAD, CW)
     dma = pltpu.SemaphoreType.DMA
-    return pl.pallas_call(
+    hidden, decoded = pl.pallas_call(
         kernel,
         out_shape=(
             jax.ShapeDtypeStruct((TOK, FEAT), BF16),
-            jax.ShapeDtypeStruct((2, 6, VAE), F32),
+            jax.ShapeDtypeStruct((6, 2, VAE), F32),
         ),
-        in_specs=[vmem, vmem, hbm, hbm, smem, hbm, vmem, vmem, vmem, hbm, vmem, vmem, vmem, hbm, hbm],
+        in_specs=[vmem, vmem, hbm, hbm, smem, hbm] + [vmem] * 7 + [hbm, vmem, vmem, vmem, hbm, hbm],
         out_specs=(vmem, vmem),
         scratch_shapes=[
             pltpu.VMEM((CH, HIST, CW), BF16),
             pltpu.VMEM((CH, HIST, CW), BF16),
-            pltpu.VMEM((FEAT, COLS), BF16),
-            pltpu.VMEM((FEAT, 64), F32),
+            pltpu.VMEM((COLS, FEAT), BF16),
+            pltpu.VMEM((64, FEAT), F32),
+            pltpu.VMEM((64, FEAT), F32),
             pltpu.VMEM((27, 16, VAE), BF16),
             pltpu.VMEM((27, VAE, VAE), BF16),
             pltpu.VMEM((CH, PAD, CW), BF16),
-            pltpu.VMEM(blocks, BF16),
-            pltpu.VMEM(blocks, BF16),
-            pltpu.VMEM(blocks, BF16),
+            pltpu.VMEM((NSEQ, PAD, CW), BF16),
+            pltpu.VMEM((CH, PLANE, PAD, CW), BF16),
+            pltpu.VMEM((CH, LINE, ROWS, CW), BF16),
             pltpu.VMEM((CH, PAD, CW), BF16),
-            pltpu.VMEM(blocks, BF16),
-            pltpu.VMEM((NSEQ, PAD, 256), BF16),
-            pltpu.VMEM((NSEQ, PAD, 256), BF16),
+            pltpu.VMEM((CH, PLANE, PAD, CW), BF16),
+            pltpu.VMEM((CH, LINE, ROWS, CW), BF16),
+            pltpu.VMEM((CH, NSEQ, PAD, CW), BF16),
+            pltpu.VMEM((CH, NSEQ, PAD, CW), BF16),
+            pltpu.VMEM((NSEQ, PAD, CW), BF16),
+            pltpu.VMEM((NSEQ, PAD, HD), BF16),
+            pltpu.VMEM((NSEQ, PAD, HD), BF16),
             pltpu.VMEM((PAD, HD), F32),
             pltpu.VMEM((3 * NSP, PAD, HD), F32),
             pltpu.VMEM((2, 8, HD), F32),
             pltpu.VMEM((9, 2, 8, HD), F32),
-            pltpu.VMEM((32, VAE), BF16),
-            pltpu.VMEM((9, 32, VAE), BF16),
+            pltpu.VMEM((2, 16, VAE), BF16),
+            pltpu.VMEM((9, 2, 16, VAE), BF16),
             pltpu.VMEM((4, 8, VAE), F32),
             pltpu.VMEM((3, 6, 16, 16), F32),
             pltpu.VMEM((3, 24, HD), F32),
@@ -575,13 +733,10 @@
             dma((CH,)),
             dma((CH,)),
             dma((4,)),
-            dma((2 + 2 * CH,)),
-            dma((CH,)),
-            dma((CH,)),
-            dma((CH,)),
-            dma((CH,)),
-            dma((CH,)),
-            dma((CH,)),
+            dma((1,)),
+        ]
+        + [dma((CH,))] * 10
+        + [
             dma,
             dma,
             dma((3 * NSP,)),
@@ -600,17 +755,22 @@
         history_keys,
         history_values,
         valid_len,
-        out_weight,
-        rows,
-        vecs,
-        biases,
-        head_weight,
-        noisy_latent,
-        prev_latent,
-        prev_feat,
+        out_weight.T,
+        attn_gate.reshape(-1, HD),
+        head_gain.reshape(-1, HD),
+        head_shift.reshape(-1, HD),
+        head_bias.reshape(1, -1),
+        conv_in_bias.reshape(-1, HD),
+        vae_gain.reshape(-1, HD),
+        conv_mid_bias.reshape(-1, HD),
+        head_weight.T,
+        noisy_latent.transpose(1, 0, 2),
+        prev_latent.transpose(0, 2, 1, 3),
+        prev_feat.transpose(0, 2, 1, 3),
         conv_in_weight.reshape(27, 16, VAE),
         conv_mid_weight.reshape(27, VAE, VAE),
     )
+    return hidden, decoded.transpose(1, 0, 2)
 
 
 def solution(mesh):

time: 103 us -> 76.4 us (0.74)
  local copies, waits for them, and re-layouts: 18.6 us -> 2.73 us
  Pallas kernels: 82.1 us -> 72 us
    pallas_call x1, Pallas kernels: 82.1 us -> 72 us  [local(): pl.pallas_call(kernel, out_shape=(jax.ShapeDtypeStruct((TOK, FEAT), BF16)...]
    unnamed x6 -> x2, local copies, waits for them, and re-layouts: 10.4 us -> 2.73 us
    another operation x12 -> x0, local copies, waits for them, and re-layouts: 4.05 us -> none  [the longest x6 2.67 us: local(): biases = jnp.stack([conv_in_bias, vae_gain, conv_mid_bias] + [none] * 5)]
    dynamic_slice x2 -> x0, local copies, waits for them, and re-layouts: 1.56 us -> none  [the longest x1 0.78 us: local(): shift = lax.dynamic_slice_in_dim(head_shift, start, FEAT, 0)]
    pallas_call x1 -> x0, local copies, waits for them, and re-layouts: 1.35 us -> none  [local(): pl.pallas_call(kernel, out_shape=(jax.ShapeDtypeStruct((TOK, FEAT), BF16)...]
    pad x1 -> x0, local copies, waits for them, and re-layouts: 1.25 us -> none  [local(): vecs = jnp.pad(head_bias[None], ((0, 7), (0, 64)))]
where the time goes in v2:
time: 76.4 us; the launch traced here: 76 us
  Pallas kernels  72 us (94%)
  local copies, waits for them, and re-layouts  2.73 us (4%)
  between operations  1.29 us (2%)
    pallas_call x1, Pallas kernels, local(): pl.pallas_call(kernel, out_shape=(jax.ShapeDtypeStruct((TOK, FEAT), BF16)...  72 us
    unnamed x2, local copies, waits for them, and re-layouts  2.73 us

profile of v2, /device:TPU:3, one launch (start us, length us, event | category | flops | bytes accessed | tf_op | source)
XLA Modules:
  0.0 76.0 jit_solution(1513129031700763224)
XLA Ops:
  1.3 72.0 %shard_map.194 = (bf16[12,1280]{1,0:T(8,128)(2,1)}, f32[6,2,384]{2,1,0:T(2,128)}) custom-call(bf16[12,1280]{1,0:T(8,128)(2,1)} %hidden_ref.1, bf16[12,1280]{1,0:T(8,128)(2,1)} %q_ref.1, bf16[2048,1280]{1,0:T(8,128)(2,1)} %k_hbm.1, bf16[2048,1280]{1,0:T(8,128)(2,1)} %v_hbm.1, s32[1]{0:T(128)S(6)} %copy.23.valid_ref, bf16[160,1280]{1,0:T(8,128)(2,1)} %bitcast.17, ...), custom_call_target="tpu_custom_call" | custom-call | tf_op jit(solution)/shard_map/pallas_call | solution.py:690
  73.3 1.4 %copy.24 = bf16[12,1280]{1,0:T(8,128)(2,1)} copy(bf16[12,1280]{1,0:T(8,128)(2,1)} %get-tuple-element.8) | data formatting | bytes 61440
  74.7 1.3 %copy.25 = f32[2,6,384]{2,0,1:T(2,128)} copy(f32[2,6,384]{2,0,1:T(2,128)} %bitcast.22) | data formatting | bytes 36864

commit v3 on v2

--- a/solution.py
+++ b/solution.py
@@ -437,11 +437,7 @@
         send_partials(c)
         if c >= 3:
             send_attention(c - 3)
-    for c in range(2, CH):
-        wait_all(rc.at[c], c_recv.at[c])
-        merge(c)
-        send_attention(c)
-        spread_attention(c - 2)
+    spread_attention(0)
 
     near(border_wait)
     win_copy.wait()
@@ -486,6 +482,16 @@
             mid += jnp.dot(window(feats, f, dy, dx, 2), wmid_s[tap], preferred_element_type=F32)
     firsts[:, 0:8, :] = first.reshape(4, 8, VAE)
 
+    def merge_and_send(c):
+        wait_all(rc.at[c], c_recv.at[c])
+        merge(c)
+        send_attention(c)
+
+    merge_and_send(2)
+    spread_attention(1)
+    merge_and_send(3)
+    spread_attention(2)
+
     gate, gain = row_of(gate_ref, 0, 10), row_of(gain_ref, 10 * p, 10)
     shift = row_of(shift_ref, 10 * p, 10)
     head_copy.wait()
@@ -500,6 +506,9 @@
     upd[...] = jnp.zeros(upd.shape, F32)
     upd[0:TOK, :] = hidden_ref[...].astype(F32)
 
+    spread_attention(3)
+    merge_and_send(LAST)
+
     w_copy.wait()
 
     def agl_ready(c):
@@ -512,7 +521,6 @@
 
     by_x = pad_rows(project(0, agl_ready(0)) + project(2, agl_ready(2)))
     by_y = project(1, agl_ready(1))
-    spread_attention(3)
     by_y = pad_rows(by_y + project(3, agl_ready(3))).reshape(4, 4, 2, PAD, COLS)
     result = by_x + jnp.stack([by_y[:, x] for x in range(4)]).reshape(NSEQ, PAD, COLS)
     wait_all(ag, d2_recv.at[LAST])
@@ -660,6 +668,11 @@
     @pl.when(jnp.logical_not(same))
     def _():
         wait_bytes(er, e_send)
+
+
+def hand_out(hidden_ref, decoded_ref, hidden_out, decoded_out):
+    hidden_out[...] = hidden_ref[...]
+    decoded_out[...] = decoded_ref[...]
 
 
 def local(
@@ -770,6 +783,15 @@
         conv_in_weight.reshape(27, 16, VAE),
         conv_mid_weight.reshape(27, VAE, VAE),
     )
+    hidden, decoded = pl.pallas_call(
+        hand_out,
+        out_shape=(
+            jax.ShapeDtypeStruct((TOK, FEAT), BF16),
+            jax.ShapeDtypeStruct((6, 2, VAE), F32),
+        ),
+        in_specs=[vmem, vmem],
+        out_specs=(vmem, vmem),
+    )(hidden, decoded)
     return hidden, decoded.transpose(1, 0, 2)
 
 

time: 76.4 us -> 74.9 us (0.980)
  local copies, waits for them, and re-layouts: 2.73 us -> 0 us
  Pallas kernels: 72 us -> 73.4 us
    unnamed x2 -> x0, local copies, waits for them, and re-layouts: 2.73 us -> none
    pallas_call x0 -> x1, Pallas kernels: none -> 1.41 us  [local(): pl.pallas_call(hand_out, out_shape=(jax.ShapeDtypeStruct((TOK, FEAT), BF1...]
where the time goes in v3:
time: 74.9 us; the launch traced here: 74.7 us
  Pallas kernels  73.4 us (98%)
  between operations  1.29 us (2%)
    pallas_call x1, Pallas kernels, local(): pl.pallas_call(kernel, out_shape=(jax.ShapeDtypeStruct((TOK, FEAT), BF16)...  72 us

profile of v3, /device:TPU:3, one launch (start us, length us, event | category | flops | bytes accessed | tf_op | source)
XLA Modules:
  0.0 74.7 jit_solution(4977780303711137196)
XLA Ops:
  1.3 72.0 %shard_map.194 = (bf16[12,1280]{1,0:T(8,128)(2,1)}, f32[6,2,384]{2,1,0:T(2,128)}) custom-call(bf16[12,1280]{1,0:T(8,128)(2,1)} %hidden_ref.1, bf16[12,1280]{1,0:T(8,128)(2,1)} %q_ref.1, bf16[2048,1280]{1,0:T(8,128)(2,1)} %k_hbm.1, bf16[2048,1280]{1,0:T(8,128)(2,1)} %v_hbm.1, s32[1]{0:T(128)S(6)} %copy.21.valid_ref, bf16[160,1280]{1,0:T(8,128)(2,1)} %bitcast.17, ...), custom_call_target="tpu_custom_call" | custom-call | tf_op jit(solution)/shard_map/pallas_call | solution.py:703
  73.2 1.4 %shard_map.195 = (bf16[12,1280]{1,0:T(8,128)(2,1)}, f32[6,2,384]{2,1,0:T(2,128)}) custom-call(bf16[12,1280]{1,0:T(8,128)(2,1)} %get-tuple-element.6.hidden_ref, f32[6,2,384]{2,1,0:T(2,128)} %get-tuple-element.7.decoded_ref), custom_call_target="tpu_custom_call" | custom-call | tf_op jit(solution)/shard_map/pallas_call | solution.py:786

commit v4 on v3

--- a/solution.py
+++ b/solution.py
@@ -142,6 +142,7 @@
     l_recv,
     f_send,
     f_recv,
+    ready,
 ):
     s = lax.axis_index("seq")
     p = lax.axis_index("sp")
@@ -159,17 +160,8 @@
 
     lax.fori_loop(1, NSEQ, greet_seq, 0)
 
-    def greet_sources(k, _):
-        greet(p * 8 + k // 3, lax.rem(p + 1 + lax.rem(k, 3), NSP))
-        return 0
-
-    lax.fori_loop(0, 24, greet_sources, 0)
-    for ds in (-1, 0, 1):
-
-        @pl.when(jnp.logical_and(s + ds >= 0, s + ds < NSEQ))
-        def _():
-            for dp in (1, 2, 3):
-                greet(s + ds, lax.rem(p + dp, NSP))
+    for dp in (1, 2, 3):
+        greet(s, lax.rem(p + dp, NSP))
 
     loads = []
     for c in range(CH):
@@ -246,8 +238,11 @@
                 fpad[2 * r + f, x, :] = pfeat_ref[f, x, r].astype(F32)
     fs[...] = fpad[...].reshape(2, 2 * 8, VAE).astype(BF16)
 
-    rows_in = 1 + jnp.where(s > 0, 1, 0) + jnp.where(s < NSEQ - 1, 1, 0)
-    pl.semaphore_wait(barrier, NSEQ - 1 + jnp.where(owner_sp != p, NSEQ, 0) + 3 * rows_in)
+    pl.semaphore_wait(barrier, NSEQ - 1 + 3)
+    for dp in (1, 2, 3):
+        pl.semaphore_signal(
+            ready, inc=1, device_id=(s, lax.rem(p + dp, NSP)), device_id_type=MESH
+        )
 
     def place(c, owner):
         if not BY_Y[c]:
@@ -316,6 +311,10 @@
         part = fr.at[slot, 0:1] if ds else fr.at[slot]
         wait_bytes(lr.at[slot], l_recv.at[slot])
         wait_bytes(part, f_recv.at[slot])
+
+    def border_left(ds, dp):
+        slot = slot_of(ds, dp)
+        part = fr.at[slot, 0:1] if ds else fr.at[slot]
         wait_bytes(lr.at[slot], l_send.at[slot])
         wait_bytes(part, f_send.at[slot])
 
@@ -426,6 +425,7 @@
 
     for c in range(1, CH):
         spread_queries(c)
+    pl.semaphore_wait(ready, 3)
     near(border_start)
     for c in range(CH):
         attend_ready(c)
@@ -599,6 +599,9 @@
     def g_wait(ds, dp):
         slot = (ds + 1) * NSP + dp
         wait_bytes(gr.at[slot], g_recv.at[slot])
+
+    def g_left(ds, dp):
+        slot = (ds + 1) * NSP + dp
         wait_bytes(gr.at[slot], g_send.at[slot])
 
     share(g_start)
@@ -650,6 +653,8 @@
     for x in range(6):
         decoded_out[x] = out[:, x, :]
 
+    near(border_left)
+    share(g_left)
     wait_all(qd, q2_send.at[0])
     for c in range(CH):
         wait_all(rc.at[c], c_send.at[c])
@@ -758,6 +763,7 @@
             dma((9,)),
             dma((9,)),
             dma((9,)),
+            pltpu.SemaphoreType.REGULAR,
         ],
         compiler_params=pltpu.CompilerParams(
             collective_id=0, has_side_effects=True, vmem_limit_bytes=56 << 20

time: 74.9 us -> 74.4 us (level)
  no operation moved by 1% of the time
where the time goes in v4:
time: 74.4 us; the launch traced here: 74.2 us
  Pallas kernels  72.9 us (98%)
  between operations  1.29 us (2%)
    pallas_call x1, Pallas kernels, local(): pl.pallas_call(kernel, out_shape=(jax.ShapeDtypeStruct((TOK, FEAT), BF16)...  71.5 us

profile of v4, /device:TPU:3, one launch (start us, length us, event | category | flops | bytes accessed | tf_op | source)
XLA Modules:
  0.0 74.2 jit_solution(6555891186357245544)
XLA Ops:
  1.3 71.5 %shard_map.194 = (bf16[12,1280]{1,0:T(8,128)(2,1)}, f32[6,2,384]{2,1,0:T(2,128)}) custom-call(bf16[12,1280]{1,0:T(8,128)(2,1)} %hidden_ref.1, bf16[12,1280]{1,0:T(8,128)(2,1)} %q_ref.1, bf16[2048,1280]{1,0:T(8,128)(2,1)} %k_hbm.1, bf16[2048,1280]{1,0:T(8,128)(2,1)} %v_hbm.1, s32[1]{0:T(128)S(6)} %copy.21.valid_ref, bf16[160,1280]{1,0:T(8,128)(2,1)} %bitcast.17, ...), custom_call_target="tpu_custom_call" | custom-call | tf_op jit(solution)/shard_map/pallas_call | solution.py:708
  72.8 1.4 %shard_map.195 = (bf16[12,1280]{1,0:T(8,128)(2,1)}, f32[6,2,384]{2,1,0:T(2,128)}) custom-call(bf16[12,1280]{1,0:T(8,128)(2,1)} %get-tuple-element.6.hidden_ref, f32[6,2,384]{2,1,0:T(2,128)} %get-tuple-element.7.decoded_ref), custom_call_target="tpu_custom_call" | custom-call | tf_op jit(solution)/shard_map/pallas_call | solution.py:792
